TPU v7x, 32 devices: a whole 2x2x4 slice. The times are simulated.
32 devices in a mesh: dp: 16 (over z, x, core), mp: 2 (over y).
Axes of the slice: x: 2, y: 2, z: 4, core: 2. Of those that a mesh axis runs over, the one named last changes fastest.
Arguments:
- tokens: bfloat16 [4096, 768], P('dp'), may hold values from -6 to 6
- w_query: bfloat16 [768, 768], P('dp', 'mp'), may hold values from -0.02734375 to 0.02734375
- w_key: bfloat16 [768, 768], P('dp', 'mp'), may hold values from -0.21875 to 0.21875
- w_value: bfloat16 [768, 768], P('dp', 'mp'), may hold values from -0.21875 to 0.21875
- w_output: bfloat16 [768, 768], P('mp', 'dp'), may hold values from -3 to 3
- bias_table: float32 [32, 12], replicated, may hold values from -6 to 6
- gain_attn: float32 [768], replicated, may hold values from 0.1 to 1.9
- gain_moe: float32 [768], replicated, may hold values from 0.1 to 1.9
- router: bfloat16 [768, 16], replicated, may hold values from -0.109375 to 0.109375
- w_in: bfloat16 [16, 768, 3072], P('dp', None, 'mp'), may hold values from -0.21875 to 0.21875
- w_out: bfloat16 [16, 3072, 768], P('dp', 'mp'), may hold values from -4 to 4
- routes: int32 [4096], P('dp'), may hold values from 0 to 15, as said below
- slots: int32 [4096], P('dp'), may hold values from 0 to 19, as said below
- buckets: int32 [511], replicated, may hold values from 0 to 31, as said below
- cotangent: bfloat16 [4096, 768], P('dp'), may hold values from -6 to 6
Outputs:
- layer_out: bfloat16 [4096, 768], P(('dp', 'mp'))
- input_grad: float32 [4096, 768], P(('dp', 'mp'))
- grad_query: float32 [768, 768], P('dp', 'mp')
- grad_key: float32 [768, 768], P('dp', 'mp')
- grad_value: float32 [768, 768], P('dp', 'mp')
- grad_output: float32 [768, 768], P('mp', 'dp')
- grad_table: float32 [32, 12], replicated
- grad_gain_attn: float32 [768], replicated
- grad_gain_moe: float32 [768], replicated
- grad_router: float32 [768, 16], replicated
- grad_w_in: float32 [16, 768, 3072], P('dp', None, 'mp')
- grad_w_out: float32 [16, 3072, 768], P('dp', 'mp')
Inputs may be any that keep to these rules, and one draw needn't show every extreme that they name: `routes`: in each sequence of 256 tokens no expert is named by more than 20 tokens, and one expert, the same in all sequences, is named by exactly 20. Within each sequence the pairs (routes, slots) are all different. `buckets`: entry k - q + 255 is the bucket of key k seen from query q.
All inputs are finite; a program needn't handle non-finite values.
Results may differ from a plain program's by a relative error of at most 0.02.
Values may be sent and summed in bfloat16 or wider, within the bound.
A program may use at most 128 MiB of HBM per device.

v0:
```python
import jax
import jax.numpy as jnp
from jax import lax
from jax.experimental import pallas as pl
from jax.experimental.pallas import tpu as pltpu
from jax.sharding import PartitionSpec as P

HEAD_DIM = 64


EPS = 1e-06
query_rows = 512


def in_blocks(array, dim, count):
    lengths = array.shape
    tiles = array.reshape(*lengths[:dim], count, lengths[dim] // count, *lengths[dim + 1 :])
    return jnp.moveaxis(tiles, dim, 0)


def sum_at_owner(array, axis, dim):
    count = lax.axis_size(axis)
    tiles = lax.all_to_all(in_blocks(array, dim, count), axis, 0, 0, tiled=True)
    return jnp.sum(tiles.astype(jnp.float32), axis=0)


def in_one_piece(arrays, axis, dim, along):
    ends, at = ([], 0)
    for a in arrays[:-1]:
        at += a.shape[along]
        ends.append(at)
    both = jnp.concatenate(arrays, axis=along)
    return tuple(jnp.split(sum_at_owner(both, axis, dim), ends, axis=along))


def normalize(inputs, gains):
    inverse = lax.rsqrt(jnp.mean(inputs * inputs, axis=-1, keepdims=True) + EPS)
    return (inputs * inverse * gains, inverse)


def norm_backward(inputs, inverse, gains, gradient):
    unit_rows = inputs * inverse
    scaled = gradient * gains
    return inverse * (scaled - unit_rows * jnp.mean(unit_rows * scaled, axis=-1, keepdims=True))


def offset_band(offset_bias, row_count, key_count):
    head_count = offset_bias.shape[0]
    window = offset_bias
    window = jnp.concatenate([window, jnp.zeros((head_count, 1), window.dtype)], axis=1)
    turned = jnp.concatenate([window[:, row_count - 1 :], window[:, : row_count - 1]], axis=1)
    span = row_count + key_count - 1
    repeated = jnp.tile(turned, (1, row_count))[:, : row_count * span]
    return repeated.reshape(head_count, row_count, span)[:, :, :key_count]


def band_sums(gradient, row_count, key_count):
    head_count = gradient.shape[0]
    padded = jnp.concatenate(
        [jnp.zeros((head_count, row_count, row_count), gradient.dtype), gradient], axis=2
    )
    flattened = jnp.concatenate(
        [padded.reshape(head_count, -1), jnp.zeros((head_count, row_count), gradient.dtype)], axis=1
    )
    skewed = flattened.reshape(head_count, row_count, row_count + key_count + 1)
    return jnp.sum(skewed, axis=1)[:, 1 : row_count + key_count]


def local(
    tokens,
    w_query,
    w_key,
    w_value,
    w_output,
    bias_table,
    gain_attn,
    gain_moe,
    router,
    w_in,
    w_out,
    routes,
    slots,
    buckets,
    cotangent,
):
    length, model_width = tokens.shape
    mp_count = lax.axis_size("mp")
    mp_rank = lax.axis_index("mp")
    own_rows = length // mp_count
    own_first = mp_rank * own_rows
    experts = router.shape[1]
    capacity = (5 * length + 4 * experts - 1) // (4 * experts)
    head_width = w_query.shape[1]
    head_count = head_width // HEAD_DIM
    row_block = min(query_rows, length)
    block_count = length // row_block
    block_starts = jnp.arange(block_count, dtype=jnp.int32) * row_block

    def own_slice(array):
        return lax.dynamic_slice_in_dim(array, own_first, own_rows, 0)

    inputs = tokens.astype(jnp.float32)
    normed_float, inverse_attn = normalize(inputs, gain_attn)
    normed_attn = normed_float.astype(jnp.bfloat16)
    full_query, full_key, full_value, full_output = (
        lax.all_gather(w_query, "dp", axis=0, tiled=True),
        lax.all_gather(w_key, "dp", axis=0, tiled=True),
        lax.all_gather(w_value, "dp", axis=0, tiled=True),
        lax.all_gather(w_output, "dp", axis=1, tiled=True),
    )
    w_joint = jnp.concatenate([full_query, full_key, full_value], axis=1)
    projected = jnp.dot(normed_attn, w_joint, preferred_element_type=jnp.float32).astype(
        jnp.bfloat16
    )
    queries = projected[:, :head_width].reshape(length, head_count, HEAD_DIM)
    keys_all = projected[:, head_width : 2 * head_width].reshape(length, head_count, HEAD_DIM)
    values = projected[:, 2 * head_width :].reshape(length, head_count, HEAD_DIM)
    bucket_hot = (
        buckets[:, None] == jnp.arange(bias_table.shape[0], dtype=jnp.int32)[None, :]
    ).astype(jnp.float32)
    table_heads = lax.dynamic_slice_in_dim(bias_table, mp_rank * head_count, head_count, 1)
    offset_bias = jnp.einsum("ob,bh->ho", bucket_hot, table_heads, precision=lax.Precision.HIGHEST)

    def attend_block(first_row):
        scores = jnp.einsum(
            "qhd,khd->hqk", queries, keys_all, preferred_element_type=jnp.float32
        ) + offset_band(offset_bias, row_block, length)
        peak_score = jnp.max(scores, axis=-1, keepdims=True)
        weights = jnp.exp(scores - peak_score)
        summed = jnp.sum(weights, axis=-1, keepdims=True)
        chances = (weights / summed).astype(jnp.bfloat16)
        context_rows = jnp.einsum(
            "hqk,khd->qhd", chances, values, preferred_element_type=jnp.float32
        )
        return (context_rows.astype(jnp.bfloat16), (peak_score + jnp.log(summed))[:, :, 0])

    context_blocks, log_totals = lax.map(attend_block, block_starts)
    context = context_blocks.reshape(length, head_width)
    partial_attn = jnp.dot(context, full_output, preferred_element_type=jnp.float32)
    attended = lax.psum(partial_attn.astype(jnp.bfloat16), "mp").astype(jnp.float32)
    residual = inputs + attended
    moe_float, inverse_moe = normalize(residual, gain_moe)
    normed_moe = moe_float.astype(jnp.bfloat16)
    logits = jnp.dot(normed_moe, router, preferred_element_type=jnp.float32)
    chance_all = jax.nn.softmax(logits, axis=-1)
    route_hot = (routes[:, None] == jnp.arange(experts, dtype=jnp.int32)[None, :]).astype(
        jnp.float32
    )
    gates = jnp.sum(chance_all * route_hot, axis=1)
    target = routes * capacity + slots
    slotted = (
        jnp.zeros((experts * capacity, model_width), jnp.bfloat16)
        .at[target]
        .set(normed_moe)
        .reshape(experts, capacity, model_width)
    )
    arrived = lax.all_to_all(slotted, "dp", split_axis=0, concat_axis=0, tiled=True)
    expert_input = arrived.reshape(-1, model_width)
    hidden_pre = jnp.dot(expert_input, w_in[0], preferred_element_type=jnp.float32)
    gelu_value, gelu_back = jax.vjp(lambda inner: jax.nn.gelu(inner, approximate=False), hidden_pre)
    hidden = gelu_value.astype(jnp.bfloat16)
    partial_out = jnp.dot(hidden, w_out[0], preferred_element_type=jnp.float32).reshape(
        arrived.shape
    )
    summed_out = lax.psum(partial_out.astype(jnp.bfloat16), "mp")
    returned = lax.all_to_all(summed_out, "dp", split_axis=0, concat_axis=0, tiled=True)
    expert_rows = returned.reshape(experts * capacity, model_width)[target].astype(jnp.float32)
    layer_full = residual + gates[:, None] * expert_rows
    layer_out = own_slice(layer_full).astype(jnp.bfloat16)
    gradient = cotangent.astype(jnp.float32)
    grad_gates = jnp.sum(gradient * expert_rows, axis=1)
    grad_rows = (gates[:, None] * gradient).astype(jnp.bfloat16)
    grad_slotted = (
        jnp.zeros((experts * capacity, model_width), jnp.bfloat16)
        .at[target]
        .set(grad_rows)
        .reshape(experts, capacity, model_width)
    )
    grad_arrived = lax.all_to_all(grad_slotted, "dp", split_axis=0, concat_axis=0, tiled=True)
    grad_expert = grad_arrived.reshape(-1, model_width)
    grad_hidden = jnp.einsum("rd,fd->rf", grad_expert, w_out[0], preferred_element_type=jnp.float32)
    grad_pre = gelu_back(grad_hidden)[0].astype(jnp.bfloat16)
    grad_w_out = jnp.einsum("rf,rd->fd", hidden, grad_expert, preferred_element_type=jnp.float32)[
        None
    ]
    grad_w_in = jnp.einsum("rd,rf->df", expert_input, grad_pre, preferred_element_type=jnp.float32)[
        None
    ]
    partial_back = jnp.einsum(
        "rf,df->rd", grad_pre, w_in[0], preferred_element_type=jnp.float32
    ).reshape(arrived.shape)
    grad_input_slots = lax.psum(partial_back.astype(jnp.bfloat16), "mp")
    grad_sent = lax.all_to_all(grad_input_slots, "dp", split_axis=0, concat_axis=0, tiled=True)
    grad_normed = grad_sent.reshape(experts * capacity, model_width)[target].astype(jnp.float32)
    grad_logits = (grad_gates[:, None] * gates[:, None] * (route_hot - chance_all)).astype(
        jnp.bfloat16
    )
    grad_normed = grad_normed + jnp.einsum(
        "se,de->sd", grad_logits, router, preferred_element_type=jnp.float32
    )
    grad_residual = gradient + norm_backward(residual, inverse_moe, gain_moe, grad_normed)
    grad_gain_moe = jnp.sum(own_slice(grad_normed) * own_slice(residual * inverse_moe), axis=0)
    grad_router = jnp.einsum(
        "sd,se->de",
        own_slice(normed_moe),
        own_slice(grad_logits),
        preferred_element_type=jnp.float32,
    )
    grad_attended = grad_residual.astype(jnp.bfloat16)
    grad_output = jnp.einsum(
        "sk,sd->kd", context, grad_attended, preferred_element_type=jnp.float32
    )
    grad_context = (
        jnp.einsum("sd,kd->sk", grad_attended, full_output, preferred_element_type=jnp.float32)
        .astype(jnp.bfloat16)
        .reshape(length, head_count, HEAD_DIM)
    )

    def back_block(running, items):
        first_row, log_total = items
        grad_keys, grad_values, grad_offsets = running
        scores = jnp.einsum(
            "qhd,khd->hqk", queries, keys_all, preferred_element_type=jnp.float32
        ) + offset_band(offset_bias, row_block, length)
        chances = jnp.exp(scores - log_total[:, :, None])
        grad_chances = jnp.einsum(
            "qhd,khd->hqk", grad_context, values, preferred_element_type=jnp.float32
        )
        grad_scores = chances * (
            grad_chances - jnp.sum(grad_chances * chances, axis=-1, keepdims=True)
        )
        grad_offsets = grad_offsets + band_sums(grad_scores, row_block, length)
        grad_low = grad_scores.astype(jnp.bfloat16)
        grad_queries = jnp.einsum(
            "hqk,khd->qhd", grad_low, keys_all, preferred_element_type=jnp.float32
        )
        grad_keys = grad_keys + jnp.einsum(
            "hqk,qhd->khd", grad_low, queries, preferred_element_type=jnp.float32
        )
        grad_values = grad_values + jnp.einsum(
            "hqk,qhd->khd",
            chances.astype(jnp.bfloat16),
            grad_context,
            preferred_element_type=jnp.float32,
        )
        return ((grad_keys, grad_values, grad_offsets), grad_queries.astype(jnp.bfloat16))

    zero_heads = jnp.zeros((length, head_count, HEAD_DIM), jnp.float32)
    zero_offsets = jnp.zeros((head_count, 2 * length - 1), jnp.float32)
    (grad_keys, grad_values, grad_offsets), grad_queries = lax.scan(
        back_block, (zero_heads, zero_heads, zero_offsets), (block_starts, log_totals)
    )
    grad_joint = jnp.concatenate(
        [
            grad_queries.reshape(length, head_width),
            grad_keys.astype(jnp.bfloat16).reshape(length, head_width),
            grad_values.astype(jnp.bfloat16).reshape(length, head_width),
        ],
        axis=1,
    )
    grad_weights = jnp.einsum(
        "sd,sk->dk", normed_attn, grad_joint, preferred_element_type=jnp.float32
    )
    grad_query, grad_key, grad_value, grad_out_proj = (
        *in_one_piece(
            (
                grad_weights[:, :head_width].astype(jnp.bfloat16),
                grad_weights[:, head_width : 2 * head_width].astype(jnp.bfloat16),
                grad_weights[:, 2 * head_width :].astype(jnp.bfloat16),
            ),
            "dp",
            0,
            1,
        ),
        sum_at_owner(grad_output.astype(jnp.bfloat16), "dp", 1),
    )
    own_grad_attn = lax.psum_scatter(
        jnp.einsum("sk,dk->sd", grad_joint, w_joint, preferred_element_type=jnp.float32).astype(
            jnp.bfloat16
        ),
        "mp",
        scatter_dimension=0,
        tiled=True,
    ).astype(jnp.float32)
    own_inputs = own_slice(inputs)
    own_inverse = own_slice(inverse_attn)
    input_grad = own_slice(grad_residual) + norm_backward(
        own_inputs, own_inverse, gain_attn, own_grad_attn
    )
    grad_gain_attn = jnp.sum(own_grad_attn * own_inputs * own_inverse, axis=0)
    table_part = jnp.einsum("ob,ho->bh", bucket_hot, grad_offsets, precision=lax.Precision.HIGHEST)
    table_full = lax.dynamic_update_slice_in_dim(
        jnp.zeros(bias_table.shape, jnp.float32), table_part, mp_rank * head_count, 1
    )
    grad_table, gain_attn_total, gain_moe_total, router_total = lax.psum(
        (table_full, grad_gain_attn, grad_gain_moe, grad_router), ("dp", "mp")
    )
    return (
        layer_out,
        input_grad,
        grad_query,
        grad_key,
        grad_value,
        grad_out_proj,
        grad_table,
        gain_attn_total,
        gain_moe_total,
        router_total,
        grad_w_in,
        grad_w_out,
    )


BF = jnp.bfloat16
F32 = jnp.float32
MESH = pl.DeviceIdType.MESH
VM = pl.BlockSpec(memory_space=pltpu.VMEM)
SLAB = 48


def params(collective_id=None):
    if collective_id is None:
        return pltpu.CompilerParams(vmem_limit_bytes=48 * 2**20)
    return pltpu.CompilerParams(
        vmem_limit_bytes=48 * 2**20, collective_id=collective_id, has_side_effects=True
    )


def dot(a, b, dims):
    return lax.dot_general(a, b, ((dims[:1], dims[1:]), ((), ())), preferred_element_type=F32)


def greet(devices):
    barrier = pltpu.get_barrier_semaphore()
    for device in devices:
        pl.semaphore_signal(barrier, inc=1, device_id=device, device_id_type=MESH)
    pl.semaphore_wait(barrier, len(devices))


def remote(src, dst, send, recv, device):
    return pltpu.make_async_remote_copy(
        src_ref=src, dst_ref=dst, send_sem=send, recv_sem=recv, device_id=device, device_id_type=MESH
    )


def place():
    dp = lax.axis_index("dp")
    return dp, lax.axis_index("mp"), dp // 4, (dp // 2) % 2, dp % 2


def gather_kernel(own_ref, out_ref, own_sem, send, recv):
    dp, mp, z, x, core = place()
    sib = dp + 1 - 2 * core
    across = dp + 2 - 4 * x
    barrier = pltpu.get_barrier_semaphore()
    for other in (sib, across):
        pl.semaphore_signal(barrier, inc=1, device_id=(other, mp), device_id_type=MESH)

    @pl.when(z > 0)
    def _():
        pl.semaphore_signal(barrier, inc=1, device_id=(dp - 4, mp), device_id_type=MESH)

    @pl.when(z < 3)
    def _():
        pl.semaphore_signal(barrier, inc=1, device_id=(dp + 4, mp), device_id_type=MESH)

    pl.semaphore_wait(barrier, 2 + jnp.minimum(z, 1) + jnp.minimum(3 - z, 1))

    def block(b):
        return out_ref.at[:, pl.ds(pl.multiple_of(b * 48, 48), 48), :]

    def copy(b, way, device, src=None):
        return remote(
            block(b) if src is None else src, block(b), send.at[way, b], recv.at[b], (device, mp)
        )

    own = pltpu.make_async_copy(own_ref, block(dp), own_sem)
    own.start()

    def spread(b, src, up, down):
        @pl.when(jnp.logical_and(up, z < 3))
        def _():
            copy(b, 0, dp + 4, src).start()

        @pl.when(jnp.logical_and(down, z > 0))
        def _():
            copy(b, 1, dp - 4, src).start()

        copy(b, 2, across, src).start()
        copy(b, 3, sib, src).start()

    spread(dp, own_ref, True, True)
    for s in (1, 2, 3):

        @pl.when(z - s >= 0)
        def _():
            b = dp - 4 * s
            copy(b, 0, sib).wait_recv()
            spread(b, None, True, False)

        @pl.when(z + s <= 3)
        def _():
            b = dp + 4 * s
            copy(b, 0, sib).wait_recv()
            spread(b, None, False, True)

    for s in range(4):
        for sign in (1, -1) if s else (1,):

            @pl.when(jnp.logical_and(z + sign * s >= 0, z + sign * s <= 3))
            def _():
                b = across + 4 * s * sign
                copy(b, 0, sib).wait_recv()
                copy(b, 3, sib).start()

    for zz in range(4):
        for xx in range(2):
            copy(zz * 4 + xx * 2 + 1 - core, 3, sib).wait_recv()
    own.wait()
    for zz in range(4):
        b = zz * 4 + x * 2 + core

        @pl.when(jnp.logical_and(zz <= z, z < 3))
        def _():
            copy(b, 0, sib).wait_send()

        @pl.when(jnp.logical_and(zz >= z, z > 0))
        def _():
            copy(b, 1, sib).wait_send()

        copy(b, 2, sib).wait_send()
        copy(b, 3, sib).wait_send()
        copy(zz * 4 + (1 - x) * 2 + core, 3, sib).wait_send()


def gather_weights(own):
    return pl.pallas_call(
        gather_kernel,
        out_shape=jax.ShapeDtypeStruct((own.shape[0], 768, own.shape[2]), BF),
        in_specs=[VM],
        out_specs=VM,
        scratch_shapes=[
            pltpu.SemaphoreType.DMA,
            pltpu.SemaphoreType.DMA((4, 16)),
            pltpu.SemaphoreType.DMA((16,)),
        ],
        compiler_params=params(1),
    )(own)


def forward_kernel(heads, tokens_ref, gain_ref, w_ref, off_ref, part_ref, normed_ref, qkv_ref, ctx_ref, p_ref):
    x = tokens_ref[...].astype(F32)
    normed = normalize(x, gain_ref[...])[0].astype(BF)
    normed_ref[...] = normed
    for j in range(3):
        qkv_ref[j] = dot(normed, w_ref[j], (1, 0)).astype(BF)
    length = x.shape[0]
    for h in range(heads):
        cols = slice(h * HEAD_DIM, (h + 1) * HEAD_DIM)
        row = jnp.broadcast_to(off_ref[h : h + 1, :], (length, 2 * length))
        bias = pltpu.roll(row, length + 1, 1, stride=1, stride_axis=0)[:, :length]
        scores = dot(qkv_ref[0, :, cols], qkv_ref[1, :, cols], (1, 1)) + bias
        weights = jnp.exp(scores - jnp.max(scores, axis=-1, keepdims=True))
        chances = weights / jnp.sum(weights, axis=-1, keepdims=True)
        p_ref[h] = chances
        ctx_ref[:, cols] = dot(chances.astype(BF), qkv_ref[2, :, cols], (1, 0)).astype(BF)
    part_ref[...] = dot(ctx_ref[...], w_ref[3], (1, 1)).astype(BF)


def backward_kernel(heads, g_ref, normed_ref, w_ref, qkv_ref, ctx_ref, p_ref, gw_ref, ga_ref, goff_ref, gc_ref, gj_ref):
    length = g_ref.shape[0]
    grad = g_ref[...]
    gw_ref[3] = dot(grad, ctx_ref[...], (0, 0)).astype(BF)
    gc_ref[...] = dot(grad, w_ref[3], (1, 0)).astype(BF)
    flip = (
        lax.broadcasted_iota(jnp.int32, (length, length), 0)
        + lax.broadcasted_iota(jnp.int32, (length, length), 1)
        == length - 1
    ).astype(F32).astype(BF)
    zeros = jnp.zeros((length, length), F32)
    goff_ref[...] = jnp.zeros_like(goff_ref)
    for h in range(heads):
        cols = slice(h * HEAD_DIM, (h + 1) * HEAD_DIM)
        chances = p_ref[h]
        gctx = gc_ref[:, cols]
        grad_chances = dot(gctx, qkv_ref[2, :, cols], (1, 1))
        grad_scores = chances * (
            grad_chances - jnp.sum(grad_chances * chances, axis=-1, keepdims=True)
        )
        high = grad_scores.astype(BF)
        rest = (grad_scores - high.astype(F32)).astype(BF)
        flipped = dot(flip, high, (1, 0)) + dot(flip, rest, (1, 0))
        skewed = pltpu.roll(
            jnp.concatenate([flipped, zeros], axis=1), 0, 1, stride=1, stride_axis=0
        )
        goff_ref[h : h + 1, :] = jnp.sum(skewed, axis=0, keepdims=True)
        gj_ref[0, :, cols] = dot(high, qkv_ref[1, :, cols], (1, 0)).astype(BF)
        gj_ref[1, :, cols] = dot(high, qkv_ref[0, :, cols], (0, 0)).astype(BF)
        gj_ref[2, :, cols] = dot(chances.astype(BF), gctx, (0, 0)).astype(BF)
    total = None
    for j in range(3):
        gw_ref[j] = dot(normed_ref[...], gj_ref[j], (0, 0)).astype(BF)
        term = dot(gj_ref[j], w_ref[j], (1, 1))
        total = term if total is None else total + term
    ga_ref[...] = total.astype(BF)


def pair_kernel(a_ref, o_ref, got, send, recv):
    dp, mp = lax.axis_index("dp"), lax.axis_index("mp")
    greet([(dp, 1 - mp)])
    c = remote(a_ref, got, send, recv, (dp, 1 - mp))
    c.start()
    c.wait()
    o_ref[...] = a_ref[...].astype(F32) + got[...].astype(F32)


def pair_sum(a):
    return pl.pallas_call(
        pair_kernel,
        out_shape=jax.ShapeDtypeStruct(a.shape, F32),
        in_specs=[VM],
        out_specs=VM,
        scratch_shapes=[pltpu.VMEM(a.shape, a.dtype), pltpu.SemaphoreType.DMA, pltpu.SemaphoreType.DMA],
        compiler_params=params(2),
    )(a)


def dispatch_kernel(slab_ref, out_ref, own_sem, send, recv, ysend, yrecv):
    dp, mp = lax.axis_index("dp"), lax.axis_index("mp")
    half = slab_ref.shape[2]
    greet([((dp + k) % 16, mp) for k in range(1, 16)] + [(dp, 1 - mp)])

    def spot(s, m):
        return out_ref.at[s, :, pl.ds(pl.multiple_of(m * half, half), half)]

    own = pltpu.make_async_copy(slab_ref.at[dp], spot(dp, mp), own_sem)
    own.start()

    def cross(k):
        s = (dp + 16 - k) % 16
        src = slab_ref.at[dp] if k == 0 else spot(s, mp)
        return remote(src, spot(s, mp), ysend.at[k], yrecv.at[k], (dp, 1 - mp))

    def direct(k):
        to = (dp + k) % 16
        return remote(slab_ref.at[to], spot(dp, mp), send.at[k], recv.at[k], (to, mp))

    for k in range(1, 16):
        direct(k).start()
    cross(0).start()
    for k in range(1, 16):
        direct(k).wait_recv()
        cross(k).start()
    for k in range(16):
        cross(k).wait()
    for k in range(1, 16):
        direct(k).wait_send()
    own.wait()


def dispatch(slab):
    return pl.pallas_call(
        dispatch_kernel,
        out_shape=jax.ShapeDtypeStruct((16, SLAB, 2 * slab.shape[2]), BF),
        in_specs=[VM],
        out_specs=VM,
        scratch_shapes=[pltpu.SemaphoreType.DMA] + [pltpu.SemaphoreType.DMA((16,))] * 4,
        compiler_params=params(3),
    )(slab)


def combine_kernel(slab_ref, out_ref, got, total, send, recv, ysend, yrecv):
    dp, mp = lax.axis_index("dp"), lax.axis_index("mp")
    half = out_ref.shape[2]
    greet([((dp + k) % 16, mp) for k in range(1, 16)] + [(dp, 1 - mp)])

    def cols(m):
        return pl.ds(pl.multiple_of(m * half, half), half)

    def cross(k):
        s = (dp + k) % 16
        return remote(
            slab_ref.at[s, :, cols(1 - mp)], got.at[s], ysend.at[k], yrecv.at[k], (dp, 1 - mp)
        )

    def direct(k):
        to = (dp + k) % 16
        return remote(total.at[to], out_ref.at[dp], send.at[k], recv.at[k], (to, mp))

    order = list(range(1, 16)) + [0]
    for k in order:
        cross(k).start()
    for k in order:
        s = (dp + k) % 16
        cross(k).wait_recv()
        summed = (slab_ref[s, :, cols(mp)].astype(F32) + got[s].astype(F32)).astype(BF)
        if k == 0:
            out_ref[s] = summed
        else:
            total[s] = summed
            direct(k).start()
    for k in range(16):
        cross(k).wait_send()
    for k in range(1, 16):
        direct(k).wait()


def combine(slab):
    shape = (16, SLAB, slab.shape[2] // 2)
    return pl.pallas_call(
        combine_kernel,
        out_shape=jax.ShapeDtypeStruct(shape, BF),
        in_specs=[VM],
        out_specs=VM,
        scratch_shapes=[pltpu.VMEM(shape, BF), pltpu.VMEM(shape, BF)]
        + [pltpu.SemaphoreType.DMA((16,))] * 4,
        compiler_params=params(4),
    )(slab)


def swap_kernel(back_ref, layer_ref, gate_ref, back_out, layer_out, gate_out, own, send, recv):
    dp, mp = lax.axis_index("dp"), lax.axis_index("mp")
    half = back_ref.shape[1]
    rows = layer_out.shape[0]
    greet([(dp, 1 - mp)])
    mine = pl.ds(pl.multiple_of(mp * half, half), half)

    def part(m):
        return layer_ref.at[pl.ds(pl.multiple_of(m * rows, rows), rows), :]

    copies = [
        remote(gate_ref, gate_out, send.at[0], recv.at[0], (dp, 1 - mp)),
        remote(back_ref, back_out.at[:, mine], send.at[1], recv.at[1], (dp, 1 - mp)),
        remote(part(1 - mp), layer_out.at[:, mine], send.at[2], recv.at[2], (dp, 1 - mp)),
        pltpu.make_async_copy(back_ref, back_out.at[:, mine], own.at[0]),
        pltpu.make_async_copy(part(mp), layer_out.at[:, mine], own.at[1]),
    ]
    for c in copies:
        c.start()
    for c in copies:
        c.wait()


def swap(back, layer, gate):
    length, half = back.shape
    return pl.pallas_call(
        swap_kernel,
        out_shape=(
            jax.ShapeDtypeStruct((length, 2 * half), BF),
            jax.ShapeDtypeStruct((length // 2, 2 * half), BF),
            jax.ShapeDtypeStruct(gate.shape, F32),
        ),
        in_specs=[VM] * 3,
        out_specs=[VM] * 3,
        scratch_shapes=[
            pltpu.SemaphoreType.DMA((2,)),
            pltpu.SemaphoreType.DMA((3,)),
            pltpu.SemaphoreType.DMA((3,)),
        ],
        compiler_params=params(5),
    )(back, layer, gate)


def reduce_kernel(gw_ref, ga_ref, sum_ref, ga_out, sib_got, x_got, up_got, down_got, acc, ga_got, sib_send, sib_recv, x_send, x_recv, z_send, z_recv, ga_send, ga_recv):
    dp, mp, z, x, core = place()
    sib = dp + 1 - 2 * core
    across = dp + 2 - 4 * x
    barrier = pltpu.get_barrier_semaphore()
    for other in ((sib, mp), (across, mp), (dp, 1 - mp)):
        pl.semaphore_signal(barrier, inc=1, device_id=other, device_id_type=MESH)

    @pl.when(z > 0)
    def _():
        pl.semaphore_signal(barrier, inc=1, device_id=(dp - 4, mp), device_id_type=MESH)

    @pl.when(z < 3)
    def _():
        pl.semaphore_signal(barrier, inc=1, device_id=(dp + 4, mp), device_id_type=MESH)

    pl.semaphore_wait(barrier, 3 + jnp.minimum(z, 1) + jnp.minimum(3 - z, 1))

    def rows(b):
        return pl.ds(pl.multiple_of(b * 48, 48), 48)

    def to_sib(xx, zz):
        b = zz * 4 + xx * 2 + 1 - core
        j = xx * 4 + zz
        return remote(
            gw_ref.at[:, rows(b), :], sib_got.at[j], sib_send.at[j], sib_recv.at[j], (sib, mp)
        )

    def to_across(zz):
        return remote(acc.at[0, zz], x_got.at[zz], x_send.at[zz], x_recv.at[zz], (across, mp))

    def to_up(zz):
        return remote(acc.at[1, zz], up_got.at[zz], z_send.at[0, zz], z_recv.at[0, zz], (dp + 4, mp))

    def to_down(zz):
        return remote(
            acc.at[1, zz], down_got.at[zz], z_send.at[1, zz], z_recv.at[1, zz], (dp - 4, mp)
        )

    half = ga_out.shape[0]
    pair = remote(
        ga_ref.at[pl.ds(pl.multiple_of((1 - mp) * half, half), half), :],
        ga_got,
        ga_send,
        ga_recv,
        (dp, 1 - mp),
    )
    order = (0, 3, 1, 2)
    for zz in order:
        to_sib(1 - x, zz).start()
    for zz in order:
        to_sib(x, zz).start()
    pair.start()

    def own(b):
        return gw_ref[:, rows(b), :].astype(F32)

    for zz in order:
        to_sib(1 - x, zz).wait_recv()
        b = zz * 4 + (1 - x) * 2 + core
        acc[0, zz] = (own(b) + sib_got[(1 - x) * 4 + zz].astype(F32)).astype(BF)
        to_across(zz).start()
    for zz in order:
        to_sib(x, zz).wait_recv()
    for zz in order:
        to_across(zz).wait_recv()
        b = zz * 4 + x * 2 + core
        part = own(b) + sib_got[x * 4 + zz].astype(F32) + x_got[zz].astype(F32)
        acc[1, zz] = part.astype(BF)

        @pl.when(jnp.logical_and(zz > z, z > 0))
        def _():
            to_up(zz).wait_recv()
            acc[1, zz] = (acc[1, zz].astype(F32) + up_got[zz].astype(F32)).astype(BF)

        @pl.when(jnp.logical_and(zz < z, z < 3))
        def _():
            to_down(zz).wait_recv()
            acc[1, zz] = (acc[1, zz].astype(F32) + down_got[zz].astype(F32)).astype(BF)

        @pl.when(zz > z)
        def _():
            to_up(zz).start()

        @pl.when(zz < z)
        def _():
            to_down(zz).start()

        @pl.when(zz == z)
        def _():
            sum_ref[...] = part

    @pl.when(z > 0)
    def _():
        to_up(z).wait_recv()
        sum_ref[...] += up_got[z].astype(F32)

    @pl.when(z < 3)
    def _():
        to_down(z).wait_recv()
        sum_ref[...] += down_got[z].astype(F32)

    pair.wait()
    ga_out[...] = (
        ga_ref[pl.ds(pl.multiple_of(mp * half, half), half), :].astype(F32)
        + ga_got[...].astype(F32)
    )
    for zz in range(4):
        to_sib(0, zz).wait_send()
        to_sib(1, zz).wait_send()
        to_across(zz).wait_send()

        @pl.when(zz > z)
        def _():
            to_up(zz).wait_send()

        @pl.when(zz < z)
        def _():
            to_down(zz).wait_send()


def reduce_weights(gw, ga):
    kinds, _, width = gw.shape
    block = (kinds, 48, width)
    half = (ga.shape[0] // 2, ga.shape[1])
    dma = pltpu.SemaphoreType.DMA
    return pl.pallas_call(
        reduce_kernel,
        out_shape=(jax.ShapeDtypeStruct(block, F32), jax.ShapeDtypeStruct(half, F32)),
        in_specs=[VM] * 2,
        out_specs=[VM] * 2,
        scratch_shapes=[
            pltpu.VMEM((8,) + block, BF),
            pltpu.VMEM((4,) + block, BF),
            pltpu.VMEM((4,) + block, BF),
            pltpu.VMEM((4,) + block, BF),
            pltpu.VMEM((2, 4) + block, BF),
            pltpu.VMEM(half, BF),
            dma((8,)),
            dma((8,)),
            dma((4,)),
            dma((4,)),
            dma((2, 4)),
            dma((2, 4)),
            dma,
            dma,
        ],
        compiler_params=params(6),
    )(gw, ga)


def total_kernel(a_ref, o_ref, got, part, send, recv, send2, recv2):
    dp, mp = lax.axis_index("dp"), lax.axis_index("mp")
    me = dp * 2 + mp

    def device(k):
        to = (me + k) % 32
        return (to // 2, to % 2)

    greet([device(k) for k in range(1, 32)])

    def first(k):
        return remote(a_ref.at[(me + k) % 32], got.at[k], send.at[k], recv.at[k], device(k))

    def second(k):
        return remote(part, o_ref.at[me], send2.at[k], recv2.at[k], device(k))

    for k in range(1, 32):
        first(k).start()
    for k in range(1, 32):
        first(k).wait_recv()
    total = a_ref[me]
    for k in range(1, 32):
        total = total + got[k]
    part[...] = total
    o_ref[me] = total
    for k in range(1, 32):
        second(k).start()
    for k in range(1, 32):
        second(k).wait()
    for k in range(1, 32):
        first(k).wait_send()


def total_everywhere(arrays):
    sizes = [a.size for a in arrays]
    flat = jnp.concatenate([a.reshape(-1) for a in arrays])
    packed = jnp.pad(flat, (0, 32 * 8 * 128 - flat.size)).reshape(32, 8, 128)
    dma = pltpu.SemaphoreType.DMA
    out = pl.pallas_call(
        total_kernel,
        out_shape=jax.ShapeDtypeStruct(packed.shape, F32),
        in_specs=[VM],
        out_specs=VM,
        scratch_shapes=[pltpu.VMEM(packed.shape, F32), pltpu.VMEM((8, 128), F32)]
        + [dma((32,))] * 4,
        compiler_params=params(7),
    )(packed).reshape(-1)
    ends, at = [], 0
    for s in sizes:
        ends.append(out[at : at + s])
        at += s
    return [e.reshape(a.shape) for e, a in zip(ends, arrays)]


def local_pairs(
    tokens,
    w_query,
    w_key,
    w_value,
    w_output,
    bias_table,
    gain_attn,
    gain_moe,
    router,
    w_in,
    w_out,
    routes,
    slots,
    buckets,
    cotangent,
):
    length, width = tokens.shape
    half_rows, half = length // 2, width // 2
    mp_rank = lax.axis_index("mp")
    experts = router.shape[1]
    capacity = (5 * length + 4 * experts - 1) // (4 * experts)
    head_width = w_query.shape[1]
    heads = head_width // HEAD_DIM

    def own_rows(array):
        return lax.dynamic_slice_in_dim(array, mp_rank * half_rows, half_rows, 0)

    def own_cols(array):
        return lax.dynamic_slice_in_dim(array, mp_rank * half, half, 1)

    weights = gather_weights(jnp.stack([w_query, w_key, w_value, w_output.T]))
    bucket_hot = (
        buckets[:, None] == jnp.arange(bias_table.shape[0], dtype=jnp.int32)[None, :]
    ).astype(F32)
    bucket_hot = jnp.pad(bucket_hot, ((0, 1), (0, 0)))
    table_heads = lax.dynamic_slice_in_dim(bias_table, mp_rank * heads, heads, 1)
    table_heads = jnp.pad(table_heads, ((0, 0), (0, 8 - heads)))
    offsets = jnp.einsum("ob,bh->ho", bucket_hot, table_heads, precision=lax.Precision.HIGHEST)
    partial, normed_attn, qkv, context, chances = pl.pallas_call(
        lambda *refs: forward_kernel(heads, *refs),
        out_shape=(
            jax.ShapeDtypeStruct((length, width), BF),
            jax.ShapeDtypeStruct((length, width), BF),
            jax.ShapeDtypeStruct((3, length, head_width), BF),
            jax.ShapeDtypeStruct((length, head_width), BF),
            jax.ShapeDtypeStruct((heads, length, length), F32),
        ),
        in_specs=[VM] * 4,
        out_specs=[VM] * 5,
        compiler_params=params(),
    )(tokens, gain_attn[None, :], weights, offsets)
    inputs = tokens.astype(F32)
    residual = inputs + pair_sum(partial)
    moe_float, inverse_moe = normalize(residual, gain_moe)
    normed_moe = moe_float.astype(BF)
    logits = jnp.dot(normed_moe, router, preferred_element_type=F32)
    chance_all = jax.nn.softmax(logits, axis=-1)
    route_hot = (routes[:, None] == jnp.arange(experts, dtype=jnp.int32)[None, :]).astype(F32)
    gates = jnp.sum(chance_all * route_hot, axis=1)
    gradient = cotangent.astype(F32)
    grad_rows = (gates[:, None] * gradient).astype(BF)
    spots = jnp.arange(experts * SLAB, dtype=jnp.int32)[:, None]
    target = (routes * SLAB + slots)[None, :]
    hot_in = (spots == target).astype(BF)
    hot_grad = (spots == target + capacity).astype(BF)
    slab = jnp.dot(
        jnp.concatenate([hot_in, hot_grad], axis=1),
        jnp.concatenate([own_cols(normed_moe), own_cols(grad_rows)], axis=0),
        preferred_element_type=F32,
    ).astype(BF)
    arrived = dispatch(slab.reshape(experts, SLAB, half))
    expert_input = arrived[:, :capacity].reshape(-1, width)
    grad_expert = arrived[:, capacity : 2 * capacity].reshape(-1, width)
    hidden_pre = jnp.dot(expert_input, w_in[0], preferred_element_type=F32)
    gelu_value, gelu_back = jax.vjp(lambda inner: jax.nn.gelu(inner, approximate=False), hidden_pre)
    hidden = gelu_value.astype(BF)
    partial_out = jnp.dot(hidden, w_out[0], preferred_element_type=F32).astype(BF)
    grad_hidden = jnp.einsum("rd,fd->rf", grad_expert, w_out[0], preferred_element_type=F32)
    grad_pre = gelu_back(grad_hidden)[0].astype(BF)
    partial_back = jnp.einsum("rf,df->rd", grad_pre, w_in[0], preferred_element_type=F32).astype(BF)
    grad_w_out = jnp.einsum("rf,rd->fd", hidden, grad_expert, preferred_element_type=F32)[None]
    grad_w_in = jnp.einsum("rd,rf->df", expert_input, grad_pre, preferred_element_type=F32)[None]
    back_slab = jnp.concatenate(
        [
            partial_out.reshape(experts, capacity, width),
            partial_back.reshape(experts, capacity, width),
            jnp.zeros((experts, SLAB - 2 * capacity, width), BF),
        ],
        axis=1,
    )
    returned = combine(back_slab).reshape(experts * SLAB, half)
    expert_rows = dot(hot_in, returned, (0, 0))
    back_half = dot(hot_grad, returned, (0, 0)).astype(BF)
    layer_half = (own_cols(residual) + gates[:, None] * expert_rows).astype(BF)
    gate_half = jnp.sum(own_cols(gradient) * expert_rows, axis=1)
    grad_slots, layer_out, gate_other = swap(
        back_half, layer_half, jnp.broadcast_to(gate_half[None, :], (8, length))
    )
    grad_gates = gate_half + gate_other[0]
    grad_logits = (grad_gates[:, None] * gates[:, None] * (route_hot - chance_all)).astype(BF)
    grad_normed = grad_slots.astype(F32) + jnp.einsum(
        "se,de->sd", grad_logits, router, preferred_element_type=F32
    )
    grad_residual = gradient + norm_backward(residual, inverse_moe, gain_moe, grad_normed)
    grad_gain_moe = jnp.sum(own_rows(grad_normed) * own_rows(residual * inverse_moe), axis=0)
    grad_router = jnp.einsum(
        "sd,se->de", own_rows(normed_moe), own_rows(grad_logits), preferred_element_type=F32
    )
    grad_weights, grad_attn, grad_offsets = pl.pallas_call(
        lambda *refs: backward_kernel(heads, *refs),
        out_shape=(
            jax.ShapeDtypeStruct(weights.shape, BF),
            jax.ShapeDtypeStruct((length, width), BF),
            jax.ShapeDtypeStruct((8, 2 * length), F32),
        ),
        in_specs=[VM] * 6,
        out_specs=[VM] * 3,
        scratch_shapes=[
            pltpu.VMEM((length, head_width), BF),
            pltpu.VMEM((3, length, head_width), BF),
        ],
        compiler_params=params(),
    )(grad_residual.astype(BF), normed_attn, weights, qkv, context, chances)
    sums, own_grad_attn = reduce_weights(grad_weights, grad_attn)
    own_inputs = own_rows(inputs)
    own_inverse = lax.rsqrt(jnp.mean(own_inputs * own_inputs, axis=-1, keepdims=True) + EPS)
    input_grad = own_rows(grad_residual) + norm_backward(
        own_inputs, own_inverse, gain_attn, own_grad_attn
    )
    grad_gain_attn = jnp.sum(own_grad_attn * own_inputs * own_inverse, axis=0)
    table_part = jnp.einsum(
        "ob,ho->bh", bucket_hot, grad_offsets, precision=lax.Precision.HIGHEST
    )[:, :heads]
    table_full = lax.dynamic_update_slice_in_dim(
        jnp.zeros(bias_table.shape, F32), table_part, mp_rank * heads, 1
    )
    grad_table, gain_attn_total, gain_moe_total, router_total = total_everywhere(
        [table_full, grad_gain_attn, grad_gain_moe, grad_router]
    )
    return (
        layer_out,
        input_grad,
        sums[0],
        sums[1],
        sums[2],
        sums[3].T,
        grad_table,
        gain_attn_total,
        gain_moe_total,
        router_total,
        grad_w_in,
        grad_w_out,
    )


def solution(mesh):
    in_specs = (
        P("dp", None),
        P("dp", "mp"),
        P("dp", "mp"),
        P("dp", "mp"),
        P("mp", "dp"),
        P(),
        P(),
        P(),
        P(),
        P("dp", None, "mp"),
        P("dp", "mp", None),
        P("dp"),
        P("dp"),
        P(),
        P("dp", None),
    )
    out_specs = (
        P(("dp", "mp"), None),
        P(("dp", "mp"), None),
        P("dp", "mp"),
        P("dp", "mp"),
        P("dp", "mp"),
        P("mp", "dp"),
        P(),
        P(),
        P(),
        P(),
        P("dp", None, "mp"),
        P("dp", "mp", None),
    )
    small = mesh.shape["mp"] == 2 and mesh.shape["dp"] == 16
    return jax.shard_map(local_pairs if small else local, mesh=mesh, in_specs=in_specs, out_specs=out_specs, check_vma=False)
```

profile of v0, /device:TPU:10, one launch (start us, length us, event | category | flops | bytes accessed | tf_op | source)
XLA Modules:
  0.0 213.2 jit_solution(6099838741703749288)
XLA Ops:
  0.7 0.9 broadcast_add_fusion
  1.5 1.0 iota_compare_fusion
  2.5 2.0 convert_element_type.56
  4.6 0.7 broadcast_in_dim.12.refs_1_
  5.2 0.8 pad_maximum_fusion.own_ref
  6.1 17.2 %shard_map.238.refs_2_ = bf16[4,768,384]{2,1,0:T(8,128)(2,1)S(1)} custom-call(bf16[4,48,384]{2,1,0:T(8,128)(2,1)S(1)} %pad_maximum_fusion.own_ref), custom_call_target="tpu_custom_call" | custom-call | tf_op jit(solution)/shard_map/pallas_call | solution.py:437
  23.4 1.4 copy-done.1
  25.2 1.7 copy-done.2
  26.8 3.3 %shard_map.239 = (bf16[256,768]{1,0:T(8,128)(2,1)S(1)}, bf16[256,768]{1,0:T(8,128)(2,1)S(1)}, bf16[3,256,384]{2,1,0:T(8,128)(2,1)S(1)}, bf16[256,384]{1,0:T(8,128)(2,1)S(1)}, f32[6,256,256]{2,1,0:T(8,128)S(1)}) custom-call(bf16[256,768]{1,0:T(8,128)(2,1)S(1)} %copy-done.3, f32[1,768]{1,0:T(1,128)S(1)} %broadcast_in_dim.12.refs_1_, ...), custom_call_target="tpu_custom_call" | custom-call | tf_op jit(solution)/shard_map/pallas_call | solution.py:908
  30.2 11.6 %shard_map.240 = f32[256,768]{1,0:T(8,128)S(1)} custom-call(bf16[256,768]{1,0:T(8,128)(2,1)S(1)} %get-tuple-element.25.a_ref), custom_call_target="tpu_custom_call" | custom-call | tf_op jit(solution)/shard_map/pallas_call | solution.py:518
  42.0 1.0 multiply_convert_fusion.1
  45.3 26.7 %shard_map.241 = bf16[16,48,768]{2,1,0:T(8,128)(2,1)S(1)} custom-call(bf16[16,48,384]{2,1,0:T(8,128)(2,1)S(1)} %bitcast.60), custom_call_target="tpu_custom_call" | custom-call | tf_op jit(solution)/shard_map/pallas_call | solution.py:562
  72.0 1.2 fusion.53
  73.2 2.0 reshape.107
  75.2 7.3 %multiply_convert_fusion = (bf16[320,1536]{1,0:T(8,128)(2,1)}, f32[320,1536]{1,0:T(8,128)}, f32[320,1536]{1,0:T(8,128)}) fusion(bf16[320,768]{1,0:T(8,128)(2,1)} %reshape.107, bf16[1,768,1536]{2,1,0:T(8,128)(2,1)S(1)} %copy-done), kind=kOutput, calls=%fused_computation.13 | convolution fusion | flops 786923520 | bytes 7766016 | tf_op jit(solution)/shard_map/dot_general | solution.py:943
  82.5 2.0 reshape.109
  84.5 4.3 %add_convert_fusion = bf16[320,1536]{1,0:T(8,128)(2,1)S(1)} fusion(f32[320,1536]{1,0:T(8,128)} %get-tuple-element.55, bf16[320,768]{1,0:T(8,128)(2,1)} %reshape.109, bf16[1,1536,768]{2,1,0:T(8,128)(2,1)} %param.25, f32[320,1536]{1,0:T(8,128)} %get-tuple-element.74), kind=kOutput, calls=%fused_computation.12 | convolution fusion | flops 761856000 | bytes 7766016 | tf_op jit(solution)/shard_map/rd,fd->rf/dot_general | solution.py:947
  88.9 1.0 copy-done.24
  89.8 1.8 fusion.23
  91.6 1.9 reshape.110
  93.6 3.7 %fusion.26 = bf16[320,768]{1,0:T(8,128)(2,1)} fusion(bf16[320,1536]{1,0:T(8,128)(2,1)} %get-tuple-element.54, bf16[1,1536,768]{2,1,0:T(8,128)(2,1)} %param.25), kind=kOutput, calls=%fused_computation.34 | convolution fusion | flops 755220480 | bytes 3833856 | tf_op jit(solution)/shard_map/dot_general | solution.py:946
  97.3 1.9 reshape.108
  99.3 1.8 maximum_maximum_fusion.slab_ref
  101.2 24.4 %shard_map.242 = bf16[16,48,384]{2,1,0:T(8,128)(2,1)S(1)} custom-call(bf16[16,48,768]{2,1,0:T(8,128)(2,1)S(1)} %maximum_maximum_fusion.slab_ref), custom_call_target="tpu_custom_call" | custom-call | tf_op jit(solution)/shard_map/pallas_call | solution.py:610
  126.6 9.7 %shard_map.243 = (bf16[256,768]{1,0:T(8,128)(2,1)S(1)}, bf16[128,768]{1,0:T(8,128)(2,1)S(1)}, f32[8,256]{1,0:T(8,128)S(1)}) custom-call(bf16[256,384]{1,0:T(8,128)(2,1)S(1)} %convolution_convert_fusion.back_ref, bf16[256,384]{1,0:T(8,128)(2,1)S(1)} %get-tuple-element.65.layer_ref, f32[8,256]{1,0:T(8,128)S(1)} %broadcast_in_dim.14.gate_ref), custom_call_target="tpu_custom_call" | custom-call | tf_op jit(solution)/shard_map/pallas_call | solution.py:646
  137.0 1.1 fusion.51
  138.1 1.4 copy-done.5
  139.5 1.1 copy-done.7
  140.6 0.9 copy-done.9
  141.5 6.1 %shard_map.244 = (bf16[4,768,384]{2,1,0:T(8,128)(2,1)S(1)}, bf16[256,768]{1,0:T(8,128)(2,1)S(1)}, f32[8,512]{1,0:T(8,128)S(1)}) custom-call(bf16[256,768]{1,0:T(8,128)(2,1)S(1)} %get-tuple-element.52.refs_0_, bf16[256,768]{1,0:T(8,128)(2,1)S(1)} %get-tuple-element.29.refs_1_, bf16[4,768,384]{2,1,0:T(8,128)(2,1)} %copy-done.1, ...), custom_call_target="tpu_custom_call" | custom-call | tf_op jit(solution)/shard_map/pallas_call | solution.py:978
  147.6 28.6 %shard_map.245 = (f32[4,48,384]{2,1,0:T(8,128)S(1)}, f32[128,768]{1,0:T(8,128)S(1)}) custom-call(bf16[4,768,384]{2,1,0:T(8,128)(2,1)S(1)} %get-tuple-element.33.gw_ref, bf16[256,768]{1,0:T(8,128)(2,1)S(1)} %get-tuple-element.34.ga_ref), custom_call_target="tpu_custom_call" | custom-call | tf_op jit(solution)/shard_map/pallas_call | solution.py:790
  176.4 0.7 multiply_reduce_fusion.3
  177.2 0.9 multiply_add_fusion.1
  178.1 0.7 slice_bitcast_fusion
  178.8 1.0 fusion.36
  179.8 1.1 reshape.113
  180.9 1.1 multiply_reduce_fusion.2
  182.0 1.2 fusion.34
  183.6 0.7 fusion.38.a_ref
  184.3 15.2 %shard_map.246 = f32[32,8,128]{2,1,0:T(8,128)S(1)} custom-call(f32[32,8,128]{2,1,0:T(8,128)S(1)} %fusion.38.a_ref), custom_call_target="tpu_custom_call" | custom-call | tf_op jit(solution)/shard_map/pallas_call | solution.py:853
  199.6 0.7 copy.30
  200.3 0.6 fusion.54
  200.9 1.3 slice.50
  202.2 1.0 slice.56
  203.2 0.8 copy.31
  204.0 4.9 %convolution_bitcast_fusion.1 = f32[1,768,1536]{2,1,0:T(8,128)} fusion(bf16[320,768]{1,0:T(8,128)(2,1)S(1)} %copy-done.21, bf16[320,1536]{1,0:T(8,128)(2,1)} %copy-done.24), kind=kOutput, calls=%fused_computation.1 | convolution fusion | flops 754974720 | bytes 6193152 | tf_op jit(solution)/shard_map/rd,rf->df/dot_general | solution.py:951
  208.9 3.6 %convolution_bitcast_fusion = f32[1,1536,768]{2,1,0:T(8,128)} fusion(bf16[320,1536]{1,0:T(8,128)(2,1)S(1)} %copy-done.52, bf16[320,768]{1,0:T(8,128)(2,1)S(1)} %copy-done.26), kind=kOutput, calls=%fused_computation | convolution fusion | flops 754974720 | bytes 6193152 | tf_op jit(solution)/shard_map/rf,rd->fd/dot_general | solution.py:950
  212.5 0.7 copy.39
  (130 shorter events, 5.1 us)
Async XLA Ops:
  0.6 74.6 %copy-start = (bf16[1,768,1536]{2,1,0:T(8,128)(2,1)S(1)}, bf16[1,768,1536]{2,1,0:T(8,128)(2,1)}, u32[]{:S(2)}) copy-start(bf16[1,768,1536]{2,1,0:T(8,128)(2,1)} %param.24) | copy-start | bytes 7077892
  1.5 1.0 copy-start.42
  1.5 1.0 copy-start.48
  2.5 22.2 %copy-start.50 = (s32[511]{0:T(512)S(1)}, s32[511]{0:T(512)}, u32[]{:S(2)}) copy-start(s32[511]{0:T(512)} %param.28) | copy-start | bytes 6136
  2.5 22.4 %copy-start.51 = (f32[32,12]{0,1:T(8,128)S(1)}, f32[32,12]{0,1:T(8,128)}, u32[]{:S(2)}) copy-start(f32[32,12]{0,1:T(8,128)} %param.20) | copy-start | bytes 4612
  2.5 22.6 %copy-start.3 = (bf16[256,768]{1,0:T(8,128)(2,1)S(1)}, bf16[256,768]{1,0:T(8,128)(2,1)}, u32[]{:S(2)}) copy-start(bf16[256,768]{1,0:T(8,128)(2,1)} %refs_0_.1) | copy-start | bytes 1179652
  23.3 1.4 copy-start.1
  24.9 16.9 %copy-start.25 = (pred[511,32]{1,0:T(8,128)(4,1)}, pred[511,32]{1,0:T(8,128)(4,1)S(1)}, u32[]{:S(2)}) copy-start(pred[511,32]{1,0:T(8,128)(4,1)S(1)} %iota_compare_fusion.2) | copy-start | bytes 49060
  25.1 1.7 copy-start.2
  30.1 13.0 %copy-start.4 = (f32[6,256,256]{2,1,0:T(8,128)}, f32[6,256,256]{2,1,0:T(8,128)S(1)}, u32[]{:S(2)}) copy-start(f32[6,256,256]{2,1,0:T(8,128)S(1)} %get-tuple-element.32.refs_5_) | copy-start | bytes 4718596
  30.1 13.0 %copy-start.6 = (bf16[3,256,384]{2,1,0:T(8,128)(2,1)}, bf16[3,256,384]{2,1,0:T(8,128)(2,1)S(1)}, u32[]{:S(2)}) copy-start(bf16[3,256,384]{2,1,0:T(8,128)(2,1)S(1)} %get-tuple-element.30.refs_3_) | copy-start | bytes 1769476
  30.1 13.0 %copy-start.8 = (bf16[256,384]{1,0:T(8,128)(2,1)}, bf16[256,384]{1,0:T(8,128)(2,1)S(1)}, u32[]{:S(2)}) copy-start(bf16[256,384]{1,0:T(8,128)(2,1)S(1)} %get-tuple-element.31.refs_4_) | copy-start | bytes 589828
  30.2 11.9 %copy-start.33 = (f32[768]{0:T(1024)S(1)}, f32[768]{0:T(1024)}, u32[]{:S(2)}) copy-start(f32[768]{0:T(1024)} %param.22) | copy-start | bytes 9220
  41.8 1.3 copy-start.29
  41.8 1.7 copy-start.46
  41.8 2.8 %copy-start.19 = (f32[256,768]{1,0:T(8,128)S(1)}, f32[256,768]{1,0:T(8,128)}, u32[]{:S(2)}) copy-start(f32[256,768]{1,0:T(8,128)} %convert_element_type.56) | copy-start | bytes 2359300
  42.0 3.3 %copy-start.14 = (f32[256,768]{1,0:T(8,128)}, f32[256,768]{1,0:T(8,128)S(1)}, u32[]{:S(2)}) copy-start(f32[256,768]{1,0:T(8,128)S(1)} %get-tuple-element.59) | copy-start | bytes 2359300
  42.0 2.7 %copy-start.27 = (pred[768,256]{1,0:T(32,128)(4,1)S(1)}, pred[768,256]{1,0:T(32,128)(4,1)}, u32[]{:S(2)}) copy-start(pred[768,256]{1,0:T(32,128)(4,1)} %get-tuple-element.77) | copy-start | bytes 589828
  42.0 2.7 %copy-start.28 = (pred[768,256]{1,0:T(32,128)(4,1)S(1)}, pred[768,256]{1,0:T(32,128)(4,1)}, u32[]{:S(2)}) copy-start(pred[768,256]{1,0:T(32,128)(4,1)} %get-tuple-element.78) | copy-start | bytes 589828
  42.0 1.4 copy-start.40
  43.1 2.2 %copy-start.17 = (bf16[256,768]{1,0:T(8,128)(2,1)}, bf16[256,768]{1,0:T(8,128)(2,1)S(1)}, u32[]{:S(2)}) copy-start(bf16[256,768]{1,0:T(8,128)(2,1)S(1)} %get-tuple-element.56) | copy-start | bytes 1179652
  88.9 1.0 copy-start.24
  99.3 26.3 %copy-start.49 = (s32[256]{0:T(256)S(1)}, s32[256]{0:T(256)}, u32[]{:S(2)}) copy-start(s32[256]{0:T(256)} %copy-done.48) | copy-start | bytes 3076
  99.3 26.7 %copy-start.15 = (f32[256,768]{1,0:T(8,128)S(1)}, f32[256,768]{1,0:T(8,128)}, u32[]{:S(2)}) copy-start(f32[256,768]{1,0:T(8,128)} %copy-done.14) | copy-start | bytes 2359300
  99.3 26.7 %copy-start.20 = (f32[256,768]{1,0:T(8,128)S(1)}, f32[256,768]{1,0:T(8,128)}, u32[]{:S(2)}) copy-start(f32[256,768]{1,0:T(8,128)} %convert_element_type.56) | copy-start | bytes 2359300
  99.3 26.7 %copy-start.37 = (f32[256]{0:T(256)S(1)}, f32[256]{0:T(256)}, u32[]{:S(2)}) copy-start(f32[256]{0:T(256)} %copy-done.36) | copy-start | bytes 3076
  99.3 26.7 %copy-start.43 = (s32[256]{0:T(256)S(1)}, s32[256]{0:T(256)}, u32[]{:S(2)}) copy-start(s32[256]{0:T(256)} %copy-done.42) | copy-start | bytes 3076
  101.1 35.2 %copy-start.39 = (f32[256]{0:T(256)S(1)}, f32[256]{0:T(256)}, u32[]{:S(2)}) copy-start(f32[256]{0:T(256)} %copy-done.38) | copy-start | bytes 3076
  101.1 35.2 %copy-start.45 = (f32[256]{0:T(256)S(1)}, f32[256]{0:T(256)}, u32[]{:S(2)}) copy-start(f32[256]{0:T(256)} %copy-done.44) | copy-start | bytes 3076
  101.1 35.2 %copy-start.47 = (s32[256]{0:T(256)S(1)}, s32[256]{0:T(256)}, u32[]{:S(2)}) copy-start(s32[256]{0:T(256)} %param.26) | copy-start | bytes 3076
  101.2 35.2 %copy-start.12 = (f32[256,768]{1,0:T(8,128)S(1)}, f32[256,768]{1,0:T(8,128)}, u32[]{:S(2)}) copy-start(f32[256,768]{1,0:T(8,128)} %get-tuple-element.57) | copy-start | bytes 2359300
  101.2 35.2 %copy-start.30 = (bf16[768,16]{0,1:T(8,128)(2,1)S(1)}, bf16[768,16]{0,1:T(8,128)(2,1)}, u32[]{:S(2)}) copy-start(bf16[768,16]{0,1:T(8,128)(2,1)} %param.23) | copy-start | bytes 73732
  101.2 35.2 %copy-start.34 = (f32[768]{0:T(1024)S(1)}, f32[768]{0:T(1024)}, u32[]{:S(2)}) copy-start(f32[768]{0:T(1024)} %param.22) | copy-start | bytes 9220
  126.1 10.9 %copy-start.23 = (bf16[256,768]{1,0:T(8,128)(2,1)S(1)}, bf16[256,768]{1,0:T(8,128)(2,1)}, u32[]{:S(2)}) copy-start(bf16[256,768]{1,0:T(8,128)(2,1)} %param.29) | copy-start | bytes 1179652
  126.1 10.9 %copy-start.41 = (f32[256]{0:T(256)S(1)}, f32[256]{0:T(256)}, u32[]{:S(2)}) copy-start(f32[256]{0:T(256)} %copy-done.40) | copy-start | bytes 3076
  136.3 1.8 copy-start.10
  136.8 1.3 copy-start.16
  138.1 1.4 copy-start.5
  139.5 1.1 copy-start.7
  147.6 28.8 %copy-start.35 = (f32[768]{0:T(1024)S(1)}, f32[768]{0:T(1024)}, u32[]{:S(2)}) copy-start(f32[768]{0:T(1024)} %param.21) | copy-start | bytes 9220
  147.6 29.6 %copy-start.22 = (f32[256,768]{1,0:T(8,128)S(1)}, f32[256,768]{1,0:T(8,128)}, u32[]{:S(2)}) copy-start(f32[256,768]{1,0:T(8,128)} %get-tuple-element.53) | copy-start | bytes 2359300
  176.3 2.5 %copy-start.18 = (bf16[256,768]{1,0:T(8,128)(2,1)S(1)}, bf16[256,768]{1,0:T(8,128)(2,1)}, u32[]{:S(2)}) copy-start(bf16[256,768]{1,0:T(8,128)(2,1)} %copy-done.17) | copy-start | bytes 1179652
  176.3 2.5 %copy-start.32 = (bf16[256,16]{0,1:T(8,128)(2,1)S(1)}, bf16[256,16]{0,1:T(8,128)(2,1)}, u32[]{:S(2)}) copy-start(bf16[256,16]{0,1:T(8,128)(2,1)} %copy-done.31) | copy-start | bytes 24580
  176.4 4.5 %copy-start.13 = (f32[256,768]{1,0:T(8,128)S(1)}, f32[256,768]{1,0:T(8,128)}, u32[]{:S(2)}) copy-start(f32[256,768]{1,0:T(8,128)} %get-tuple-element.57) | copy-start | bytes 2359300
  182.0 22.0 %copy-start.21 = (bf16[320,768]{1,0:T(8,128)(2,1)S(1)}, bf16[320,768]{1,0:T(8,128)(2,1)}, u32[]{:S(2)}) copy-start(bf16[320,768]{1,0:T(8,128)(2,1)} %reshape.107) | copy-start | bytes 1474564
  204.0 4.9 %copy-start.26 = (bf16[320,768]{1,0:T(8,128)(2,1)S(1)}, bf16[320,768]{1,0:T(8,128)(2,1)}, u32[]{:S(2)}) copy-start(bf16[320,768]{1,0:T(8,128)(2,1)} %reshape.109) | copy-start | bytes 1474564
  204.0 4.9 %copy-start.52 = (bf16[320,1536]{1,0:T(8,128)(2,1)S(1)}, bf16[320,1536]{1,0:T(8,128)(2,1)}, u32[]{:S(2)}) copy-start(bf16[320,1536]{1,0:T(8,128)(2,1)} %get-tuple-element.54) | copy-start | bytes 2949124
  208.9 3.6 %copy-start.11 = (bf16[128,768]{1,0:T(8,128)(2,1)S(1)}, bf16[128,768]{1,0:T(8,128)(2,1)}, u32[]{:S(2)}) copy-start(bf16[128,768]{1,0:T(8,128)(2,1)} %copy-done.10) | copy-start | bytes 589828
  (5 other events, 3.2 us)
where the time goes:
time: 217 us; the launch traced here: 213 us
  Pallas kernels  143 us (66%)
  matrix products  30.3 us (14%)
  local copies, waits for them, and re-layouts  26.1 us (12%)
  other arithmetic  12.7 us (6%)
    pallas_call x1, Pallas kernels, reduce_weights(): pl.pallas_call(reduce_kernel, out_shape=(jax.ShapeDtypeStruct(block, F32)...  28.6 us
    pallas_call x1, Pallas kernels, dispatch(): pl.pallas_call(dispatch_kernel, out_shape=jax.ShapeDtypeStruct((16, SLAB,...  26.7 us
    pallas_call x1, Pallas kernels, combine(): pl.pallas_call(combine_kernel, out_shape=jax.ShapeDtypeStruct(shape, BF),...  24.4 us
    pallas_call x1, Pallas kernels, gather_weights(): pl.pallas_call(gather_kernel, out_shape=jax.ShapeDtypeStruct((own.shape[0...  17.2 us
    pallas_call x1, Pallas kernels, total_everywhere(): pl.pallas_call(total_kernel, out_shape=jax.ShapeDtypeStruct(packed.shape,...  15.2 us
    pallas_call x1, Pallas kernels, pair_sum(): pl.pallas_call(pair_kernel, out_shape=jax.ShapeDtypeStruct(a.shape, F32),...  11.6 us
    unnamed x109, local copies, waits for them, and re-layouts  11 us
    pallas_call x1, Pallas kernels, swap(): pl.pallas_call(swap_kernel, out_shape=(jax.ShapeDtypeStruct((length, 2 *...  9.66 us

commit v1 on v0

--- a/solution.py
+++ b/solution.py
@@ -569,6 +569,70 @@
     )(slab)
 
 
+def expert_kernel(capacity, arrived_ref, w_in_ref, w_out_ref, slab_ref, gin_ref, gout_ref, x_ref, g_ref, out_ref, back_ref):
+    step, last = pl.program_id(0), pl.num_programs(0) - 1
+    packed = x_ref.shape[0]
+    count = packed // capacity
+
+    def chooser(first):
+        row = lax.broadcasted_iota(jnp.int32, (packed, count * SLAB), 0)
+        col = lax.broadcasted_iota(jnp.int32, (packed, count * SLAB), 1)
+        return (col == row + row // capacity * (SLAB - capacity) + first).astype(F32).astype(BF)
+
+    @pl.when(step == 0)
+    def _():
+        x_ref[...] = dot(chooser(0), arrived_ref[...], (1, 0)).astype(BF)
+        g_ref[...] = dot(chooser(capacity), arrived_ref[...], (1, 0)).astype(BF)
+        out_ref[...] = jnp.zeros_like(out_ref)
+        back_ref[...] = jnp.zeros_like(back_ref)
+
+    pre = dot(x_ref[...], w_in_ref[0], (1, 0))
+    share = 0.5 * (1.0 + lax.erf(pre * (0.5**0.5)))
+    hidden = (pre * share).astype(BF)
+    slope = share + pre * jnp.exp(-0.5 * pre * pre) * ((0.5 / jnp.pi) ** 0.5)
+    out_ref[...] += dot(hidden, w_out_ref[0], (1, 0))
+    grad_pre = (slope * dot(g_ref[...], w_out_ref[0], (1, 1))).astype(BF)
+    back_ref[...] += dot(grad_pre, w_in_ref[0], (1, 1))
+    gout_ref[0] = dot(hidden, g_ref[...], (0, 0))
+    gin_ref[0] = dot(x_ref[...], grad_pre, (0, 0))
+
+    @pl.when(step == last)
+    def _():
+        slab_ref[...] = (
+            dot(chooser(0), out_ref[...].astype(BF), (0, 0))
+            + dot(chooser(capacity), back_ref[...].astype(BF), (0, 0))
+        ).astype(BF)
+
+
+def expert_layer(arrived, w_in, w_out, capacity):
+    count, _, width = arrived.shape
+    inner = w_in.shape[2]
+    tile = 256
+    packed = count * capacity
+    whole = pl.BlockSpec((count * SLAB, width), lambda i: (0, 0))
+    in_tile = pl.BlockSpec((1, width, tile), lambda i: (0, 0, i))
+    out_tile = pl.BlockSpec((1, tile, width), lambda i: (0, i, 0))
+    slab, gin, gout = pl.pallas_call(
+        lambda *refs: expert_kernel(capacity, *refs),
+        grid=(inner // tile,),
+        out_shape=(
+            jax.ShapeDtypeStruct((count * SLAB, width), BF),
+            jax.ShapeDtypeStruct(w_in.shape, F32),
+            jax.ShapeDtypeStruct(w_out.shape, F32),
+        ),
+        in_specs=[whole, in_tile, out_tile],
+        out_specs=(whole, in_tile, out_tile),
+        scratch_shapes=[
+            pltpu.VMEM((packed, width), BF),
+            pltpu.VMEM((packed, width), BF),
+            pltpu.VMEM((packed, width), F32),
+            pltpu.VMEM((packed, width), F32),
+        ],
+        compiler_params=params(),
+    )(arrived.reshape(count * SLAB, width), w_in, w_out)
+    return slab.reshape(arrived.shape), gin, gout
+
+
 def combine_kernel(slab_ref, out_ref, got, total, send, recv, ysend, yrecv):
     dp, mp = lax.axis_index("dp"), lax.axis_index("mp")
     half = out_ref.shape[2]
@@ -661,23 +725,21 @@
     )(back, layer, gate)
 
 
-def reduce_kernel(gw_ref, ga_ref, sum_ref, ga_out, sib_got, x_got, up_got, down_got, acc, ga_got, sib_send, sib_recv, x_send, x_recv, z_send, z_recv, ga_send, ga_recv):
+def reduce_kernel(gw_ref, ga_ref, few_ref, sum_ref, ga_out, few_out, sib_got, x_got, up_got, down_got, acc, ga_got, sib_send, sib_recv, x_send, x_recv, z_send, z_recv, ga_send, ga_recv, few_got, few_part, few_mate, few_total, f1_send, f1_recv, f2_send, f2_recv, y_send, y_recv):
     dp, mp, z, x, core = place()
     sib = dp + 1 - 2 * core
     across = dp + 2 - 4 * x
-    barrier = pltpu.get_barrier_semaphore()
-    for other in ((sib, mp), (across, mp), (dp, 1 - mp)):
-        pl.semaphore_signal(barrier, inc=1, device_id=other, device_id_type=MESH)
-
-    @pl.when(z > 0)
-    def _():
-        pl.semaphore_signal(barrier, inc=1, device_id=(dp - 4, mp), device_id_type=MESH)
-
-    @pl.when(z < 3)
-    def _():
-        pl.semaphore_signal(barrier, inc=1, device_id=(dp + 4, mp), device_id_type=MESH)
-
-    pl.semaphore_wait(barrier, 3 + jnp.minimum(z, 1) + jnp.minimum(3 - z, 1))
+    greet([((dp + k) % 16, mp) for k in range(1, 16)] + [(dp, 1 - mp)])
+
+    def scatter(k):
+        to = (dp + k) % 16
+        return remote(few_ref.at[to], few_got.at[k], f1_send.at[k], f1_recv.at[k], (to, mp))
+
+    def collect(k):
+        to = (dp + k) % 16
+        return remote(few_total, few_out.at[dp], f2_send.at[k], f2_recv.at[k], (to, mp))
+
+    mate = remote(few_part, few_mate, y_send, y_recv, (dp, 1 - mp))
 
     def rows(b):
         return pl.ds(pl.multiple_of(b * 48, 48), 48)
@@ -714,6 +776,8 @@
     for zz in order:
         to_sib(x, zz).start()
     pair.start()
+    for k in range(1, 16):
+        scatter(k).start()
 
     def own(b):
         return gw_ref[:, rows(b), :].astype(F32)
@@ -723,6 +787,12 @@
         b = zz * 4 + (1 - x) * 2 + core
         acc[0, zz] = (own(b) + sib_got[(1 - x) * 4 + zz].astype(F32)).astype(BF)
         to_across(zz).start()
+    total = few_ref[dp]
+    for k in range(1, 16):
+        scatter(k).wait_recv()
+        total = total + few_got[k]
+    few_part[...] = total
+    mate.start()
     for zz in order:
         to_sib(x, zz).wait_recv()
     for zz in order:
@@ -753,6 +823,12 @@
         def _():
             sum_ref[...] = part
 
+    mate.wait()
+    few_total[...] = few_part[...] + few_mate[...]
+    few_out[dp] = few_total[...]
+    for k in range(1, 16):
+        collect(k).start()
+
     @pl.when(z > 0)
     def _():
         to_up(z).wait_recv()
@@ -780,18 +856,28 @@
         @pl.when(zz < z)
         def _():
             to_down(zz).wait_send()
-
-
-def reduce_weights(gw, ga):
+    for k in range(1, 16):
+        scatter(k).wait_send()
+        collect(k).wait()
+
+
+def reduce_weights(gw, ga, arrays):
     kinds, _, width = gw.shape
     block = (kinds, 48, width)
     half = (ga.shape[0] // 2, ga.shape[1])
+    flat = jnp.concatenate([a.reshape(-1) for a in arrays])
+    rows = -(-flat.size // (16 * 8 * 128)) * 8
+    few = jnp.pad(flat, (0, 16 * rows * 128 - flat.size)).reshape(16, rows, 128)
     dma = pltpu.SemaphoreType.DMA
-    return pl.pallas_call(
+    sums, ga_sum, out = pl.pallas_call(
         reduce_kernel,
-        out_shape=(jax.ShapeDtypeStruct(block, F32), jax.ShapeDtypeStruct(half, F32)),
-        in_specs=[VM] * 2,
-        out_specs=[VM] * 2,
+        out_shape=(
+            jax.ShapeDtypeStruct(block, F32),
+            jax.ShapeDtypeStruct(half, F32),
+            jax.ShapeDtypeStruct(few.shape, F32),
+        ),
+        in_specs=[VM] * 3,
+        out_specs=[VM] * 3,
         scratch_shapes=[
             pltpu.VMEM((8,) + block, BF),
             pltpu.VMEM((4,) + block, BF),
@@ -807,63 +893,25 @@
             dma((2, 4)),
             dma,
             dma,
+            pltpu.VMEM(few.shape, F32),
+            pltpu.VMEM((rows, 128), F32),
+            pltpu.VMEM((rows, 128), F32),
+            pltpu.VMEM((rows, 128), F32),
+            dma((16,)),
+            dma((16,)),
+            dma((16,)),
+            dma((16,)),
+            dma,
+            dma,
         ],
         compiler_params=params(6),
-    )(gw, ga)
-
-
-def total_kernel(a_ref, o_ref, got, part, send, recv, send2, recv2):
-    dp, mp = lax.axis_index("dp"), lax.axis_index("mp")
-    me = dp * 2 + mp
-
-    def device(k):
-        to = (me + k) % 32
-        return (to // 2, to % 2)
-
-    greet([device(k) for k in range(1, 32)])
-
-    def first(k):
-        return remote(a_ref.at[(me + k) % 32], got.at[k], send.at[k], recv.at[k], device(k))
-
-    def second(k):
-        return remote(part, o_ref.at[me], send2.at[k], recv2.at[k], device(k))
-
-    for k in range(1, 32):
-        first(k).start()
-    for k in range(1, 32):
-        first(k).wait_recv()
-    total = a_ref[me]
-    for k in range(1, 32):
-        total = total + got[k]
-    part[...] = total
-    o_ref[me] = total
-    for k in range(1, 32):
-        second(k).start()
-    for k in range(1, 32):
-        second(k).wait()
-    for k in range(1, 32):
-        first(k).wait_send()
-
-
-def total_everywhere(arrays):
-    sizes = [a.size for a in arrays]
-    flat = jnp.concatenate([a.reshape(-1) for a in arrays])
-    packed = jnp.pad(flat, (0, 32 * 8 * 128 - flat.size)).reshape(32, 8, 128)
-    dma = pltpu.SemaphoreType.DMA
-    out = pl.pallas_call(
-        total_kernel,
-        out_shape=jax.ShapeDtypeStruct(packed.shape, F32),
-        in_specs=[VM],
-        out_specs=VM,
-        scratch_shapes=[pltpu.VMEM(packed.shape, F32), pltpu.VMEM((8, 128), F32)]
-        + [dma((32,))] * 4,
-        compiler_params=params(7),
-    )(packed).reshape(-1)
+    )(gw, ga, few)
+    out = out.reshape(-1)
     ends, at = [], 0
-    for s in sizes:
-        ends.append(out[at : at + s])
-        at += s
-    return [e.reshape(a.shape) for e, a in zip(ends, arrays)]
+    for a in arrays:
+        ends.append(out[at : at + a.size].reshape(a.shape))
+        at += a.size
+    return sums, ga_sum, ends
 
 
 def local_pairs(
@@ -938,25 +986,7 @@
         preferred_element_type=F32,
     ).astype(BF)
     arrived = dispatch(slab.reshape(experts, SLAB, half))
-    expert_input = arrived[:, :capacity].reshape(-1, width)
-    grad_expert = arrived[:, capacity : 2 * capacity].reshape(-1, width)
-    hidden_pre = jnp.dot(expert_input, w_in[0], preferred_element_type=F32)
-    gelu_value, gelu_back = jax.vjp(lambda inner: jax.nn.gelu(inner, approximate=False), hidden_pre)
-    hidden = gelu_value.astype(BF)
-    partial_out = jnp.dot(hidden, w_out[0], preferred_element_type=F32).astype(BF)
-    grad_hidden = jnp.einsum("rd,fd->rf", grad_expert, w_out[0], preferred_element_type=F32)
-    grad_pre = gelu_back(grad_hidden)[0].astype(BF)
-    partial_back = jnp.einsum("rf,df->rd", grad_pre, w_in[0], preferred_element_type=F32).astype(BF)
-    grad_w_out = jnp.einsum("rf,rd->fd", hidden, grad_expert, preferred_element_type=F32)[None]
-    grad_w_in = jnp.einsum("rd,rf->df", expert_input, grad_pre, preferred_element_type=F32)[None]
-    back_slab = jnp.concatenate(
-        [
-            partial_out.reshape(experts, capacity, width),
-            partial_back.reshape(experts, capacity, width),
-            jnp.zeros((experts, SLAB - 2 * capacity, width), BF),
-        ],
-        axis=1,
-    )
+    back_slab, grad_w_in, grad_w_out = expert_layer(arrived, w_in, w_out, capacity)
     returned = combine(back_slab).reshape(experts * SLAB, half)
     expert_rows = dot(hot_in, returned, (0, 0))
     back_half = dot(hot_grad, returned, (0, 0)).astype(BF)
@@ -990,21 +1020,21 @@
         ],
         compiler_params=params(),
     )(grad_residual.astype(BF), normed_attn, weights, qkv, context, chances)
-    sums, own_grad_attn = reduce_weights(grad_weights, grad_attn)
-    own_inputs = own_rows(inputs)
-    own_inverse = lax.rsqrt(jnp.mean(own_inputs * own_inputs, axis=-1, keepdims=True) + EPS)
-    input_grad = own_rows(grad_residual) + norm_backward(
-        own_inputs, own_inverse, gain_attn, own_grad_attn
-    )
-    grad_gain_attn = jnp.sum(own_grad_attn * own_inputs * own_inverse, axis=0)
+    inverse_attn = lax.rsqrt(jnp.mean(inputs * inputs, axis=-1, keepdims=True) + EPS)
+    grad_gain_attn = jnp.sum(grad_attn.astype(F32) * inputs * inverse_attn, axis=0)
     table_part = jnp.einsum(
         "ob,ho->bh", bucket_hot, grad_offsets, precision=lax.Precision.HIGHEST
     )[:, :heads]
     table_full = lax.dynamic_update_slice_in_dim(
         jnp.zeros(bias_table.shape, F32), table_part, mp_rank * heads, 1
     )
-    grad_table, gain_attn_total, gain_moe_total, router_total = total_everywhere(
-        [table_full, grad_gain_attn, grad_gain_moe, grad_router]
+    sums, own_grad_attn, (grad_table, gain_attn_total, gain_moe_total, router_total) = (
+        reduce_weights(
+            grad_weights, grad_attn, [table_full, grad_gain_attn, grad_gain_moe, grad_router]
+        )
+    )
+    input_grad = own_rows(grad_residual) + norm_backward(
+        own_rows(inputs), own_rows(inverse_attn), gain_attn, own_grad_attn
     )
     return (
         layer_out,

time: 217 us -> 167 us (0.77)
  matrix products: 30.3 us -> 3 us
  local copies, waits for them, and re-layouts: 26.1 us -> 7.63 us
  other arithmetic: 12.7 us -> 9.63 us
    dot_general x6 -> x0, matrix products: 25.7 us -> none  [the longest x1 7.31 us: local_pairs(): hidden_pre = jnp.dot(expert_input, w_in[0], preferred_element_type=F32)]
    reshape x7 -> x3, local copies, waits for them, and re-layouts: 9.18 us -> 0.35 us  [the longest x2 0.26 us: reduce_weights(): flat = jnp.concatenate([a.reshape(-1) for a in arrays])]
    unnamed x109 -> x41, local copies, waits for them, and re-layouts: 11 us -> 4.01 us
    slice x5 -> x4, local copies, waits for them, and re-layouts: 4.14 us -> 0.81 us  [reduce_weights(): ends.append(out[at:at + a.size].reshape(a.shape))]
    pallas_call x1, Pallas kernels: 28.6 us -> 30.9 us  [reduce_weights(): pl.pallas_call(reduce_kernel, out_shape=(jax.ShapeDtypeStruct(block, F32)...]
where the time goes in v1:
time: 167 us; the launch traced here: 164 us
  Pallas kernels  143 us (86%)
  other arithmetic  9.63 us (6%)
  local copies, waits for them, and re-layouts  7.63 us (5%)
  matrix products  3 us (2%)
    pallas_call x1, Pallas kernels, reduce_weights(): pl.pallas_call(reduce_kernel, out_shape=(jax.ShapeDtypeStruct(block, F32)...  30.9 us
    pallas_call x1, Pallas kernels, dispatch(): pl.pallas_call(dispatch_kernel, out_shape=jax.ShapeDtypeStruct((16, SLAB,...  26.7 us
    pallas_call x1, Pallas kernels, combine(): pl.pallas_call(combine_kernel, out_shape=jax.ShapeDtypeStruct(shape, BF),...  24.2 us
    pallas_call x1, Pallas kernels, gather_weights(): pl.pallas_call(gather_kernel, out_shape=jax.ShapeDtypeStruct((own.shape[0...  17.2 us
    pallas_call x1, Pallas kernels, expert_layer(): pl.pallas_call(lambda *refs: expert_kernel(capacity, *refs), grid=(inner...  13.2 us
    pallas_call x1, Pallas kernels, pair_sum(): pl.pallas_call(pair_kernel, out_shape=jax.ShapeDtypeStruct(a.shape, F32),...  11.5 us
    pallas_call x1, Pallas kernels, swap(): pl.pallas_call(swap_kernel, out_shape=(jax.ShapeDtypeStruct((length, 2 *...  9.63 us
    pallas_call x1, Pallas kernels, local_pairs(): pl.pallas_call(lambda *refs: backward_kernel(heads, *refs), out_shape=(ja...  6.14 us

profile of v1, /device:TPU:10, one launch (start us, length us, event | category | flops | bytes accessed | tf_op | source)
XLA Modules:
  0.0 164.2 jit_solution(13790708481302007779)
XLA Ops:
  0.7 0.7 broadcast_add_fusion
  1.4 0.7 broadcast_in_dim.6.refs_1_
  2.1 0.7 constant_dynamic-slice_fusion.1
  2.8 0.8 iota_compare_fusion.2
  3.6 0.2 fusion.10.refs_3_
  3.8 0.9 pad_maximum_fusion.own_ref
  4.7 0.2 iota_compare_fusion
  4.9 1.1 convert_element_type.47
  6.0 1.9 %convert_element_type.45 = f32[256,768]{1,0:T(8,128)} convert(bf16[256,768]{1,0:T(8,128)(2,1)} %refs_0_.1) | non-fusion elementwise | flops 196608 | bytes 1179648 | tf_op jit(solution)/shard_map/convert_element_type | solution.py:969
  8.0 17.2 %shard_map.238.refs_2_ = bf16[4,768,384]{2,1,0:T(8,128)(2,1)S(1)} custom-call(bf16[4,48,384]{2,1,0:T(8,128)(2,1)S(1)} %pad_maximum_fusion.own_ref), custom_call_target="tpu_custom_call" | custom-call | tf_op jit(solution)/shard_map/pallas_call | solution.py:437
  25.2 3.3 %shard_map.239 = (bf16[256,768]{1,0:T(8,128)(2,1)S(1)}, bf16[256,768]{1,0:T(8,128)(2,1)S(1)}, bf16[3,256,384]{2,1,0:T(8,128)(2,1)S(1)}, bf16[256,384]{1,0:T(8,128)(2,1)S(1)}, f32[6,256,256]{2,1,0:T(8,128)S(1)}) custom-call(bf16[256,768]{1,0:T(8,128)(2,1)S(1)} %copy-done.2, f32[1,768]{1,0:T(1,128)S(1)} %broadcast_in_dim.6.refs_1_, ...), custom_call_target="tpu_custom_call" | custom-call | tf_op jit(solution)/shard_map/pallas_call | solution.py:956
  28.5 1.1 copy-done.4
  29.7 11.5 %shard_map.240 = f32[256,768]{1,0:T(8,128)S(1)} custom-call(bf16[256,768]{1,0:T(8,128)(2,1)S(1)} %get-tuple-element.29.a_ref), custom_call_target="tpu_custom_call" | custom-call | tf_op jit(solution)/shard_map/pallas_call | solution.py:518
  41.2 0.2 multiply_reduce_fusion.3
  41.5 0.1 dynamic-slice.3
  41.5 1.0 multiply_convert_fusion
  42.6 0.3 fusion.31
  42.9 0.1 multiply_convert_fusion.1
  43.1 0.6 fusion.4
  43.7 26.7 %shard_map.241 = bf16[16,48,768]{2,1,0:T(8,128)(2,1)S(1)} custom-call(bf16[16,48,384]{2,1,0:T(8,128)(2,1)S(1)} %bitcast.34), custom_call_target="tpu_custom_call" | custom-call | tf_op jit(solution)/shard_map/pallas_call | solution.py:562
  70.4 13.2 %shard_map.242 = (bf16[768,768]{1,0:T(8,128)(2,1)S(1)}, f32[1,768,1536]{2,1,0:T(8,128)}, f32[1,1536,768]{2,1,0:T(8,128)}) custom-call(bf16[768,768]{1,0:T(8,128)(2,1)S(1)} %bitcast.30, bf16[1,768,1536]{2,1,0:T(8,128)(2,1)S(1)} %copy-done.3, bf16[1,1536,768]{2,1,0:T(8,128)(2,1)} %refs_2_.1), custom_call_target="tpu_custom_call" | custom-call | tf_op jit(solution)/shard_map/pallas_call | solution.py:615
  83.6 24.2 %shard_map.243 = bf16[16,48,384]{2,1,0:T(8,128)(2,1)S(1)} custom-call(bf16[16,48,768]{2,1,0:T(8,128)(2,1)S(1)} %bitcast.33), custom_call_target="tpu_custom_call" | custom-call | tf_op jit(solution)/shard_map/pallas_call | solution.py:674
  107.9 0.5 multiply_reduce_fusion.6
  108.4 0.4 convolution_convert_fusion.back_ref
  108.8 9.6 %shard_map.244 = (bf16[256,768]{1,0:T(8,128)(2,1)S(1)}, bf16[128,768]{1,0:T(8,128)(2,1)S(1)}, f32[8,256]{1,0:T(8,128)S(1)}) custom-call(bf16[256,384]{1,0:T(8,128)(2,1)S(1)} %convolution_convert_fusion.back_ref, bf16[256,384]{1,0:T(8,128)(2,1)S(1)} %get-tuple-element.68.layer_ref, f32[8,256]{1,0:T(8,128)S(1)} %broadcast_in_dim.7.gate_ref), custom_call_target="tpu_custom_call" | custom-call | tf_op jit(solution)/shard_map/pallas_call | solution.py:710
  118.5 0.2 fusion.14
  118.8 0.2 reshape.120
  118.9 0.4 multiply_reduce_fusion.2
  119.4 0.1 multiply_reduce_fusion.5
  119.5 1.2 fusion.29
  120.6 0.4 copy-done.5
  121.0 0.2 copy-done.7
  121.2 0.1 copy-done.9
  121.3 6.1 %shard_map.245 = (bf16[4,768,384]{2,1,0:T(8,128)(2,1)S(1)}, bf16[256,768]{1,0:T(8,128)(2,1)S(1)}, f32[8,512]{1,0:T(8,128)S(1)}) custom-call(bf16[256,768]{1,0:T(8,128)(2,1)S(1)} %get-tuple-element.58.refs_0_, bf16[256,768]{1,0:T(8,128)(2,1)S(1)} %copy-done.9, bf16[4,768,384]{2,1,0:T(8,128)(2,1)} %copy-done.1, bf16[3,256,384]{2,1,0:T(8,128)(2,1)S(1)} %copy-done.7, ...), custom_call_target="tpu_custom_call" | custom-call | tf_op jit(solution)/shard_map/pallas_call | solution.py:1008
  127.4 0.4 fusion.12
  127.8 0.2 dynamic_update_slice.3
  128.0 0.1 reshape.119
  128.2 0.2 multiply_reduce_fusion
  128.3 30.9 %shard_map.246 = (f32[4,48,384]{2,1,0:T(8,128)S(1)}, f32[128,768]{1,0:T(8,128)S(1)}, f32[16,8,128]{2,1,0:T(8,128)S(1)}) custom-call(bf16[4,768,384]{2,1,0:T(8,128)(2,1)S(1)} %get-tuple-element.38.gw_ref, bf16[256,768]{1,0:T(8,128)(2,1)S(1)} %get-tuple-element.39.ga_ref, f32[16,8,128]{2,1,0:T(8,128)S(1)} %fusion.16.few_ref), custom_call_target="tpu_custom_call" | custom-call | tf_op jit(solution)/shard_map/pallas_call | solution.py:872
  159.3 0.7 slice_bitcast_fusion
  160.0 0.2 multiply_reduce_fusion.4
  160.2 0.9 multiply_add_fusion.1
  161.1 0.6 fusion.30
  161.7 0.1 reshape.123
  161.8 0.7 copy.30
  162.5 0.2 slice.42
  162.7 0.8 copy.31
  163.5 0.7 copy.39
  (48 shorter events, 0.3 us)
Async XLA Ops:
  0.6 41.9 %copy-start = (bf16[768,16]{0,1:T(8,128)(2,1)S(1)}, bf16[768,16]{0,1:T(8,128)(2,1)}, u32[]{:S(2)}) copy-start(bf16[768,16]{0,1:T(8,128)(2,1)} %param.23) | copy-start | bytes 73732
  4.9 20.2 %copy-start.2 = (bf16[256,768]{1,0:T(8,128)(2,1)S(1)}, bf16[256,768]{1,0:T(8,128)(2,1)}, u32[]{:S(2)}) copy-start(bf16[256,768]{1,0:T(8,128)(2,1)} %refs_0_.1) | copy-start | bytes 1179652
  25.2 16.3 %copy-start.1 = (bf16[4,768,384]{2,1,0:T(8,128)(2,1)}, bf16[4,768,384]{2,1,0:T(8,128)(2,1)S(1)}, u32[]{:S(2)}) copy-start(bf16[4,768,384]{2,1,0:T(8,128)(2,1)S(1)} %shard_map.238.refs_2_) | copy-start | bytes 7077892
  25.2 16.4 %copy-start.16 = (f32[768]{0:T(1024)S(1)}, f32[768]{0:T(1024)}, u32[]{:S(2)}) copy-start(f32[768]{0:T(1024)} %param.22) | copy-start | bytes 9220
  28.5 1.1 copy-start.4
  29.7 12.9 %copy-start.6 = (bf16[3,256,384]{2,1,0:T(8,128)(2,1)}, bf16[3,256,384]{2,1,0:T(8,128)(2,1)S(1)}, u32[]{:S(2)}) copy-start(bf16[3,256,384]{2,1,0:T(8,128)(2,1)S(1)} %get-tuple-element.35.refs_3_) | copy-start | bytes 1769476
  29.7 12.9 %copy-start.8 = (bf16[256,768]{1,0:T(8,128)(2,1)}, bf16[256,768]{1,0:T(8,128)(2,1)S(1)}, u32[]{:S(2)}) copy-start(bf16[256,768]{1,0:T(8,128)(2,1)S(1)} %get-tuple-element.34.refs_1_) | copy-start | bytes 1179652
  41.2 1.7 %copy-start.18 = (s32[256]{0:T(256)S(1)}, s32[256]{0:T(256)}, u32[]{:S(2)}) copy-start(s32[256]{0:T(256)} %param.26) | copy-start | bytes 3076
  43.0 27.4 %copy-start.3 = (bf16[1,768,1536]{2,1,0:T(8,128)(2,1)S(1)}, bf16[1,768,1536]{2,1,0:T(8,128)(2,1)}, u32[]{:S(2)}) copy-start(bf16[1,768,1536]{2,1,0:T(8,128)(2,1)} %refs_1_.1) | copy-start | bytes 7077892
  107.8 11.1 %copy-start.12 = (f32[256,768]{1,0:T(8,128)S(1)}, f32[256,768]{1,0:T(8,128)}, u32[]{:S(2)}) copy-start(f32[256,768]{1,0:T(8,128)} %get-tuple-element.61) | copy-start | bytes 2359300
  108.8 10.6 %copy-start.15 = (bf16[256,768]{1,0:T(8,128)(2,1)S(1)}, bf16[256,768]{1,0:T(8,128)(2,1)}, u32[]{:S(2)}) copy-start(bf16[256,768]{1,0:T(8,128)(2,1)} %param.29) | copy-start | bytes 1179652
  118.5 2.2 %copy-start.10 = (bf16[128,768]{1,0:T(8,128)(2,1)}, bf16[128,768]{1,0:T(8,128)(2,1)S(1)}, u32[]{:S(2)}) copy-start(bf16[128,768]{1,0:T(8,128)(2,1)S(1)} %get-tuple-element.95) | copy-start | bytes 589828
  119.3 1.7 %copy-start.5 = (f32[6,256,256]{2,1,0:T(8,128)S(1)}, f32[6,256,256]{2,1,0:T(8,128)}, u32[]{:S(2)}) copy-start(f32[6,256,256]{2,1,0:T(8,128)} %copy-done.4) | copy-start | bytes 4718596
  119.3 1.8 %copy-start.7 = (bf16[3,256,384]{2,1,0:T(8,128)(2,1)S(1)}, bf16[3,256,384]{2,1,0:T(8,128)(2,1)}, u32[]{:S(2)}) copy-start(bf16[3,256,384]{2,1,0:T(8,128)(2,1)} %copy-done.6) | copy-start | bytes 1769476
  119.4 1.9 %copy-start.9 = (bf16[256,768]{1,0:T(8,128)(2,1)S(1)}, bf16[256,768]{1,0:T(8,128)(2,1)}, u32[]{:S(2)}) copy-start(bf16[256,768]{1,0:T(8,128)(2,1)} %copy-done.8) | copy-start | bytes 1179652
  127.4 32.6 %copy-start.17 = (f32[768]{0:T(1024)S(1)}, f32[768]{0:T(1024)}, u32[]{:S(2)}) copy-start(f32[768]{0:T(1024)} %param.21) | copy-start | bytes 9220
  128.1 31.9 %copy-start.13 = (f32[256,768]{1,0:T(8,128)S(1)}, f32[256,768]{1,0:T(8,128)}, u32[]{:S(2)}) copy-start(f32[256,768]{1,0:T(8,128)} %convert_element_type.45) | copy-start | bytes 2359300
  128.3 31.9 %copy-start.14 = (f32[256,768]{1,0:T(8,128)S(1)}, f32[256,768]{1,0:T(8,128)}, u32[]{:S(2)}) copy-start(f32[256,768]{1,0:T(8,128)} %get-tuple-element.59) | copy-start | bytes 2359300
  159.3 4.2 %copy-start.11 = (bf16[128,768]{1,0:T(8,128)(2,1)S(1)}, bf16[128,768]{1,0:T(8,128)(2,1)}, u32[]{:S(2)}) copy-start(bf16[128,768]{1,0:T(8,128)(2,1)} %copy-done.10) | copy-start | bytes 589828

commit v2 on v1

--- a/solution.py
+++ b/solution.py
@@ -530,6 +530,9 @@
     half = slab_ref.shape[2]
     greet([((dp + k) % 16, mp) for k in range(1, 16)] + [(dp, 1 - mp)])
 
+    def peer(k):
+        return dp + sum(bit * (1 - 2 * (dp // bit % 2)) for bit in (1, 2, 4, 8) if k & bit)
+
     def spot(s, m):
         return out_ref.at[s, :, pl.ds(pl.multiple_of(m * half, half), half)]
 
@@ -537,15 +540,15 @@
     own.start()
 
     def cross(k):
-        s = (dp + 16 - k) % 16
+        s = peer(k)
         src = slab_ref.at[dp] if k == 0 else spot(s, mp)
         return remote(src, spot(s, mp), ysend.at[k], yrecv.at[k], (dp, 1 - mp))
 
     def direct(k):
-        to = (dp + k) % 16
+        to = peer(k)
         return remote(slab_ref.at[to], spot(dp, mp), send.at[k], recv.at[k], (to, mp))
 
-    for k in range(1, 16):
+    for k in (8, 1, 12, 2, 9, 3, 13, 4, 10, 5, 14, 6, 11, 7, 15):
         direct(k).start()
     cross(0).start()
     for k in range(1, 16):
@@ -638,24 +641,27 @@
     half = out_ref.shape[2]
     greet([((dp + k) % 16, mp) for k in range(1, 16)] + [(dp, 1 - mp)])
 
+    def peer(k):
+        return dp + sum(bit * (1 - 2 * (dp // bit % 2)) for bit in (1, 2, 4, 8) if k & bit)
+
     def cols(m):
         return pl.ds(pl.multiple_of(m * half, half), half)
 
     def cross(k):
-        s = (dp + k) % 16
+        s = peer(k)
         return remote(
             slab_ref.at[s, :, cols(1 - mp)], got.at[s], ysend.at[k], yrecv.at[k], (dp, 1 - mp)
         )
 
     def direct(k):
-        to = (dp + k) % 16
+        to = peer(k)
         return remote(total.at[to], out_ref.at[dp], send.at[k], recv.at[k], (to, mp))
 
-    order = list(range(1, 16)) + [0]
+    order = (12, 8, 13, 9, 14, 10, 15, 11, 4, 5, 6, 7, 2, 3, 1, 0)
     for k in order:
         cross(k).start()
     for k in order:
-        s = (dp + k) % 16
+        s = peer(k)
         cross(k).wait_recv()
         summed = (slab_ref[s, :, cols(mp)].astype(F32) + got[s].astype(F32)).astype(BF)
         if k == 0:
@@ -682,22 +688,15 @@
     )(slab)
 
 
-def swap_kernel(back_ref, layer_ref, gate_ref, back_out, layer_out, gate_out, own, send, recv):
+def swap_kernel(back_ref, gate_ref, back_out, gate_out, own, send, recv):
     dp, mp = lax.axis_index("dp"), lax.axis_index("mp")
     half = back_ref.shape[1]
-    rows = layer_out.shape[0]
     greet([(dp, 1 - mp)])
-    mine = pl.ds(pl.multiple_of(mp * half, half), half)
-
-    def part(m):
-        return layer_ref.at[pl.ds(pl.multiple_of(m * rows, rows), rows), :]
-
+    mine = back_out.at[:, pl.ds(pl.multiple_of(mp * half, half), half)]
     copies = [
         remote(gate_ref, gate_out, send.at[0], recv.at[0], (dp, 1 - mp)),
-        remote(back_ref, back_out.at[:, mine], send.at[1], recv.at[1], (dp, 1 - mp)),
-        remote(part(1 - mp), layer_out.at[:, mine], send.at[2], recv.at[2], (dp, 1 - mp)),
-        pltpu.make_async_copy(back_ref, back_out.at[:, mine], own.at[0]),
-        pltpu.make_async_copy(part(mp), layer_out.at[:, mine], own.at[1]),
+        remote(back_ref, mine, send.at[1], recv.at[1], (dp, 1 - mp)),
+        pltpu.make_async_copy(back_ref, mine, own),
     ]
     for c in copies:
         c.start()
@@ -705,27 +704,26 @@
         c.wait()
 
 
-def swap(back, layer, gate):
+def swap(back, gate):
     length, half = back.shape
     return pl.pallas_call(
         swap_kernel,
         out_shape=(
             jax.ShapeDtypeStruct((length, 2 * half), BF),
-            jax.ShapeDtypeStruct((length // 2, 2 * half), BF),
             jax.ShapeDtypeStruct(gate.shape, F32),
         ),
-        in_specs=[VM] * 3,
-        out_specs=[VM] * 3,
+        in_specs=[VM] * 2,
+        out_specs=[VM] * 2,
         scratch_shapes=[
+            pltpu.SemaphoreType.DMA,
             pltpu.SemaphoreType.DMA((2,)),
-            pltpu.SemaphoreType.DMA((3,)),
-            pltpu.SemaphoreType.DMA((3,)),
+            pltpu.SemaphoreType.DMA((2,)),
         ],
         compiler_params=params(5),
-    )(back, layer, gate)
-
-
-def reduce_kernel(gw_ref, ga_ref, few_ref, sum_ref, ga_out, few_out, sib_got, x_got, up_got, down_got, acc, ga_got, sib_send, sib_recv, x_send, x_recv, z_send, z_recv, ga_send, ga_recv, few_got, few_part, few_mate, few_total, f1_send, f1_recv, f2_send, f2_recv, y_send, y_recv):
+    )(back, gate)
+
+
+def reduce_kernel(gw_ref, ga_ref, few_ref, layer_ref, sum_ref, ga_out, few_out, layer_out, sib_got, x_got, up_got, down_got, acc, ga_got, sib_send, sib_recv, x_send, x_recv, z_send, z_recv, ga_send, ga_recv, few_got, few_part, few_mate, few_total, f1_send, f1_recv, f2_send, f2_recv, y_send, y_recv, own_sem):
     dp, mp, z, x, core = place()
     sib = dp + 1 - 2 * core
     across = dp + 2 - 4 * x
@@ -766,18 +764,33 @@
     pair = remote(
         ga_ref.at[pl.ds(pl.multiple_of((1 - mp) * half, half), half), :],
         ga_got,
-        ga_send,
-        ga_recv,
+        ga_send.at[0],
+        ga_recv.at[0],
         (dp, 1 - mp),
     )
+    lines = pl.ds(pl.multiple_of(mp * layer_ref.shape[1], layer_ref.shape[1]), layer_ref.shape[1])
+    swap_layer = remote(
+        layer_ref.at[pl.ds(pl.multiple_of((1 - mp) * half, half), half), :],
+        layer_out.at[:, lines],
+        ga_send.at[1],
+        ga_recv.at[1],
+        (dp, 1 - mp),
+    )
+    own_layer = pltpu.make_async_copy(
+        layer_ref.at[pl.ds(pl.multiple_of(mp * half, half), half), :],
+        layer_out.at[:, lines],
+        own_sem,
+    )
+    for k in range(1, 16):
+        scatter(k).start()
     order = (0, 3, 1, 2)
     for zz in order:
         to_sib(1 - x, zz).start()
     for zz in order:
         to_sib(x, zz).start()
     pair.start()
-    for k in range(1, 16):
-        scatter(k).start()
+    swap_layer.start()
+    own_layer.start()
 
     def own(b):
         return gw_ref[:, rows(b), :].astype(F32)
@@ -795,6 +808,11 @@
     mate.start()
     for zz in order:
         to_sib(x, zz).wait_recv()
+    mate.wait()
+    few_total[...] = few_part[...] + few_mate[...]
+    few_out[dp] = few_total[...]
+    for k in range(1, 16):
+        collect(k).start()
     for zz in order:
         to_across(zz).wait_recv()
         b = zz * 4 + x * 2 + core
@@ -823,12 +841,6 @@
         def _():
             sum_ref[...] = part
 
-    mate.wait()
-    few_total[...] = few_part[...] + few_mate[...]
-    few_out[dp] = few_total[...]
-    for k in range(1, 16):
-        collect(k).start()
-
     @pl.when(z > 0)
     def _():
         to_up(z).wait_recv()
@@ -840,6 +852,8 @@
         sum_ref[...] += down_got[z].astype(F32)
 
     pair.wait()
+    swap_layer.wait()
+    own_layer.wait()
     ga_out[...] = (
         ga_ref[pl.ds(pl.multiple_of(mp * half, half), half), :].astype(F32)
         + ga_got[...].astype(F32)
@@ -861,7 +875,7 @@
         collect(k).wait()
 
 
-def reduce_weights(gw, ga, arrays):
+def reduce_weights(gw, ga, layer, arrays):
     kinds, _, width = gw.shape
     block = (kinds, 48, width)
     half = (ga.shape[0] // 2, ga.shape[1])
@@ -869,15 +883,16 @@
     rows = -(-flat.size // (16 * 8 * 128)) * 8
     few = jnp.pad(flat, (0, 16 * rows * 128 - flat.size)).reshape(16, rows, 128)
     dma = pltpu.SemaphoreType.DMA
-    sums, ga_sum, out = pl.pallas_call(
+    sums, ga_sum, out, layer_out = pl.pallas_call(
         reduce_kernel,
         out_shape=(
             jax.ShapeDtypeStruct(block, F32),
             jax.ShapeDtypeStruct(half, F32),
             jax.ShapeDtypeStruct(few.shape, F32),
+            jax.ShapeDtypeStruct(half, BF),
         ),
-        in_specs=[VM] * 3,
-        out_specs=[VM] * 3,
+        in_specs=[VM] * 4,
+        out_specs=[VM] * 4,
         scratch_shapes=[
             pltpu.VMEM((8,) + block, BF),
             pltpu.VMEM((4,) + block, BF),
@@ -891,8 +906,8 @@
             dma((4,)),
             dma((2, 4)),
             dma((2, 4)),
-            dma,
-            dma,
+            dma((2,)),
+            dma((2,)),
             pltpu.VMEM(few.shape, F32),
             pltpu.VMEM((rows, 128), F32),
             pltpu.VMEM((rows, 128), F32),
@@ -903,15 +918,16 @@
             dma((16,)),
             dma,
             dma,
+            dma,
         ],
         compiler_params=params(6),
-    )(gw, ga, few)
+    )(gw, ga, few, layer)
     out = out.reshape(-1)
     ends, at = [], 0
     for a in arrays:
         ends.append(out[at : at + a.size].reshape(a.shape))
         at += a.size
-    return sums, ga_sum, ends
+    return sums, ga_sum, ends, layer_out
 
 
 def local_pairs(
@@ -992,8 +1008,8 @@
     back_half = dot(hot_grad, returned, (0, 0)).astype(BF)
     layer_half = (own_cols(residual) + gates[:, None] * expert_rows).astype(BF)
     gate_half = jnp.sum(own_cols(gradient) * expert_rows, axis=1)
-    grad_slots, layer_out, gate_other = swap(
-        back_half, layer_half, jnp.broadcast_to(gate_half[None, :], (8, length))
+    grad_slots, gate_other = swap(
+        back_half, jnp.broadcast_to(gate_half[None, :], (8, length))
     )
     grad_gates = gate_half + gate_other[0]
     grad_logits = (grad_gates[:, None] * gates[:, None] * (route_hot - chance_all)).astype(BF)
@@ -1028,11 +1044,13 @@
     table_full = lax.dynamic_update_slice_in_dim(
         jnp.zeros(bias_table.shape, F32), table_part, mp_rank * heads, 1
     )
-    sums, own_grad_attn, (grad_table, gain_attn_total, gain_moe_total, router_total) = (
-        reduce_weights(
-            grad_weights, grad_attn, [table_full, grad_gain_attn, grad_gain_moe, grad_router]
-        )
-    )
+    sums, own_grad_attn, few, layer_out = reduce_weights(
+        grad_weights,
+        grad_attn,
+        layer_half,
+        [table_full, grad_gain_attn, grad_gain_moe, grad_router],
+    )
+    grad_table, gain_attn_total, gain_moe_total, router_total = few
     input_grad = own_rows(grad_residual) + norm_backward(
         own_rows(inputs), own_rows(inverse_attn), gain_attn, own_grad_attn
     )

time: 167 us -> 160 us (0.958); the launches traced: 164 us -> 160 us
  Pallas kernels: 143 us -> 139 us
    pallas_call x1, Pallas kernels: 24.2 us -> 21.1 us  [combine(): pl.pallas_call(combine_kernel, out_shape=jax.ShapeDtypeStruct(shape, BF),...]
    pallas_call x1, Pallas kernels: 9.63 us -> 7.18 us  [swap(): pl.pallas_call(swap_kernel, out_shape=(jax.ShapeDtypeStruct((length, 2 *...]
    pallas_call x1, Pallas kernels: 30.9 us -> 32.8 us  [reduce_weights(): pl.pallas_call(reduce_kernel, out_shape=(jax.ShapeDtypeStruct(block, F32)...]
    unnamed x41 -> x45, local copies, waits for them, and re-layouts: 4.01 us -> 4.05 us
where the time goes in v2:
time: 160 us
  Pallas kernels  139 us (87%)
  other arithmetic  9.66 us (6%)
  local copies, waits for them, and re-layouts  7.67 us (5%)
  matrix products  2.99 us (2%)
    pallas_call x1, Pallas kernels, reduce_weights(): pl.pallas_call(reduce_kernel, out_shape=(jax.ShapeDtypeStruct(block, F32)...  32.8 us
    pallas_call x1, Pallas kernels, dispatch(): pl.pallas_call(dispatch_kernel, out_shape=jax.ShapeDtypeStruct((16, SLAB,...  26.1 us
    pallas_call x1, Pallas kernels, combine(): pl.pallas_call(combine_kernel, out_shape=jax.ShapeDtypeStruct(shape, BF),...  21.1 us
    pallas_call x1, Pallas kernels, gather_weights(): pl.pallas_call(gather_kernel, out_shape=jax.ShapeDtypeStruct((own.shape[0...  17.2 us
    pallas_call x1, Pallas kernels, expert_layer(): pl.pallas_call(lambda *refs: expert_kernel(capacity, *refs), grid=(inner...  13.2 us
    pallas_call x1, Pallas kernels, pair_sum(): pl.pallas_call(pair_kernel, out_shape=jax.ShapeDtypeStruct(a.shape, F32),...  11.5 us
    pallas_call x1, Pallas kernels, swap(): pl.pallas_call(swap_kernel, out_shape=(jax.ShapeDtypeStruct((length, 2 *...  7.18 us
    pallas_call x1, Pallas kernels, local_pairs(): pl.pallas_call(lambda *refs: backward_kernel(heads, *refs), out_shape=(ja...  6.14 us

profile of v2, /device:TPU:10, one launch (start us, length us, event | category | flops | bytes accessed | tf_op | source)
XLA Modules:
  0.0 160.0 jit_solution(16341958348126509973)
XLA Ops:
  0.7 0.7 broadcast_add_fusion
  1.4 0.7 broadcast_in_dim.6.refs_1_
  2.1 0.7 constant_dynamic-slice_fusion.1
  2.8 0.8 iota_compare_fusion.2
  3.6 0.2 fusion.10.refs_3_
  3.8 0.9 pad_maximum_fusion.own_ref
  4.7 0.2 iota_compare_fusion
  4.9 1.1 convert_element_type.45
  6.0 1.9 %convert_element_type.46 = f32[256,768]{1,0:T(8,128)} convert(bf16[256,768]{1,0:T(8,128)(2,1)} %refs_0_.1) | non-fusion elementwise | flops 196608 | bytes 1179648 | tf_op jit(solution)/shard_map/convert_element_type | solution.py:985
  8.0 17.2 %shard_map.238.refs_2_ = bf16[4,768,384]{2,1,0:T(8,128)(2,1)S(1)} custom-call(bf16[4,48,384]{2,1,0:T(8,128)(2,1)S(1)} %pad_maximum_fusion.own_ref), custom_call_target="tpu_custom_call" | custom-call | tf_op jit(solution)/shard_map/pallas_call | solution.py:437
  25.2 3.3 %shard_map.239 = (bf16[256,768]{1,0:T(8,128)(2,1)S(1)}, bf16[256,768]{1,0:T(8,128)(2,1)S(1)}, bf16[3,256,384]{2,1,0:T(8,128)(2,1)S(1)}, bf16[256,384]{1,0:T(8,128)(2,1)S(1)}, f32[6,256,256]{2,1,0:T(8,128)S(1)}) custom-call(bf16[256,768]{1,0:T(8,128)(2,1)S(1)} %copy-done.2, f32[1,768]{1,0:T(1,128)S(1)} %broadcast_in_dim.6.refs_1_, ...), custom_call_target="tpu_custom_call" | custom-call | tf_op jit(solution)/shard_map/pallas_call | solution.py:972
  28.5 1.1 copy-done.4
  29.7 11.5 %shard_map.240 = f32[256,768]{1,0:T(8,128)S(1)} custom-call(bf16[256,768]{1,0:T(8,128)(2,1)S(1)} %get-tuple-element.29.a_ref), custom_call_target="tpu_custom_call" | custom-call | tf_op jit(solution)/shard_map/pallas_call | solution.py:518
  41.2 0.2 multiply_reduce_fusion.3
  41.4 0.1 dynamic-slice.3
  41.5 1.1 multiply_convert_fusion
  42.6 0.3 fusion.31
  42.9 0.1 multiply_convert_fusion.1
  43.1 0.6 fusion.4
  43.7 26.1 %shard_map.241 = bf16[16,48,768]{2,1,0:T(8,128)(2,1)S(1)} custom-call(bf16[16,48,384]{2,1,0:T(8,128)(2,1)S(1)} %bitcast.34), custom_call_target="tpu_custom_call" | custom-call | tf_op jit(solution)/shard_map/pallas_call | solution.py:565
  69.8 13.2 %shard_map.242 = (bf16[768,768]{1,0:T(8,128)(2,1)S(1)}, f32[1,768,1536]{2,1,0:T(8,128)}, f32[1,1536,768]{2,1,0:T(8,128)}) custom-call(bf16[768,768]{1,0:T(8,128)(2,1)S(1)} %bitcast.30, bf16[1,768,1536]{2,1,0:T(8,128)(2,1)S(1)} %copy-done.3, bf16[1,1536,768]{2,1,0:T(8,128)(2,1)} %refs_2_.1), custom_call_target="tpu_custom_call" | custom-call | tf_op jit(solution)/shard_map/pallas_call | solution.py:618
  83.0 21.1 %shard_map.243 = bf16[16,48,384]{2,1,0:T(8,128)(2,1)S(1)} custom-call(bf16[16,48,768]{2,1,0:T(8,128)(2,1)S(1)} %bitcast.33), custom_call_target="tpu_custom_call" | custom-call | tf_op jit(solution)/shard_map/pallas_call | solution.py:680
  104.1 0.5 add_convert_fusion
  104.7 0.4 convolution_convert_fusion.back_ref
  105.1 7.2 %shard_map.244 = (bf16[256,768]{1,0:T(8,128)(2,1)S(1)}, f32[8,256]{1,0:T(8,128)S(1)}) custom-call(bf16[256,384]{1,0:T(8,128)(2,1)S(1)} %convolution_convert_fusion.back_ref, f32[8,256]{1,0:T(8,128)S(1)} %broadcast_in_dim.7.gate_ref), custom_call_target="tpu_custom_call" | custom-call | tf_op jit(solution)/shard_map/pallas_call | solution.py:709
  112.3 0.2 fusion.14
  112.6 0.2 reshape.120
  112.8 0.4 multiply_reduce_fusion.2
  113.2 0.1 multiply_reduce_fusion.5
  113.3 1.2 fusion.29
  114.4 0.3 copy-done.5
  114.8 0.2 copy-done.7
  115.0 0.1 copy-done.9
  115.1 6.1 %shard_map.245 = (bf16[4,768,384]{2,1,0:T(8,128)(2,1)S(1)}, bf16[256,768]{1,0:T(8,128)(2,1)S(1)}, f32[8,512]{1,0:T(8,128)S(1)}) custom-call(bf16[256,768]{1,0:T(8,128)(2,1)S(1)} %get-tuple-element.58.refs_0_, bf16[256,768]{1,0:T(8,128)(2,1)S(1)} %copy-done.9, bf16[4,768,384]{2,1,0:T(8,128)(2,1)} %copy-done.1, bf16[3,256,384]{2,1,0:T(8,128)(2,1)S(1)} %copy-done.7, ...), custom_call_target="tpu_custom_call" | custom-call | tf_op jit(solution)/shard_map/pallas_call | solution.py:1024
  121.3 0.4 fusion.12
  121.7 0.2 dynamic_update_slice.3
  121.9 0.1 reshape.119
  122.0 0.2 multiply_reduce_fusion
  122.2 32.8 %shard_map.246 = (f32[4,48,384]{2,1,0:T(8,128)S(1)}, f32[128,768]{1,0:T(8,128)S(1)}, f32[16,8,128]{2,1,0:T(8,128)S(1)}, bf16[128,768]{1,0:T(8,128)(2,1)S(1)}) custom-call(bf16[4,768,384]{2,1,0:T(8,128)(2,1)S(1)} %get-tuple-element.37.gw_ref, bf16[256,768]{1,0:T(8,128)(2,1)S(1)} %get-tuple-element.38.ga_ref, f32[16,8,128]{2,1,0:T(8,128)S(1)} %fusion.16.few_ref, ...), custom_call_target="tpu_custom_call" | custom-call | tf_op jit(solution)/shard_map/pallas_call | solution.py:886
  155.1 0.2 multiply_reduce_fusion.4
  155.3 0.9 multiply_add_fusion.1
  156.2 0.6 fusion.30
  156.8 0.1 reshape.123
  156.9 0.7 copy.30
  157.6 0.7 slice_bitcast_fusion
  158.3 0.2 slice.42
  158.5 0.8 copy.31
  159.3 0.7 copy.39
  (52 shorter events, 0.3 us)
Async XLA Ops:
  0.6 42.0 %copy-start = (bf16[768,16]{0,1:T(8,128)(2,1)S(1)}, bf16[768,16]{0,1:T(8,128)(2,1)}, u32[]{:S(2)}) copy-start(bf16[768,16]{0,1:T(8,128)(2,1)} %param.23) | copy-start | bytes 73732
  4.9 20.2 %copy-start.2 = (bf16[256,768]{1,0:T(8,128)(2,1)S(1)}, bf16[256,768]{1,0:T(8,128)(2,1)}, u32[]{:S(2)}) copy-start(bf16[256,768]{1,0:T(8,128)(2,1)} %refs_0_.1) | copy-start | bytes 1179652
  25.2 16.3 %copy-start.1 = (bf16[4,768,384]{2,1,0:T(8,128)(2,1)}, bf16[4,768,384]{2,1,0:T(8,128)(2,1)S(1)}, u32[]{:S(2)}) copy-start(bf16[4,768,384]{2,1,0:T(8,128)(2,1)S(1)} %shard_map.238.refs_2_) | copy-start | bytes 7077892
  25.2 16.4 %copy-start.18 = (f32[768]{0:T(1024)S(1)}, f32[768]{0:T(1024)}, u32[]{:S(2)}) copy-start(f32[768]{0:T(1024)} %param.22) | copy-start | bytes 9220
  28.5 1.2 copy-start.4
  29.7 12.9 %copy-start.6 = (bf16[3,256,384]{2,1,0:T(8,128)(2,1)}, bf16[3,256,384]{2,1,0:T(8,128)(2,1)S(1)}, u32[]{:S(2)}) copy-start(bf16[3,256,384]{2,1,0:T(8,128)(2,1)S(1)} %get-tuple-element.34.refs_3_) | copy-start | bytes 1769476
  29.7 12.9 %copy-start.8 = (bf16[256,768]{1,0:T(8,128)(2,1)}, bf16[256,768]{1,0:T(8,128)(2,1)S(1)}, u32[]{:S(2)}) copy-start(bf16[256,768]{1,0:T(8,128)(2,1)S(1)} %get-tuple-element.33.refs_1_) | copy-start | bytes 1179652
  29.7 12.9 %copy-start.10 = (bf16[256,384]{1,0:T(8,128)(2,1)}, bf16[256,384]{1,0:T(8,128)(2,1)S(1)}, u32[]{:S(2)}) copy-start(bf16[256,384]{1,0:T(8,128)(2,1)S(1)} %get-tuple-element.35.refs_4_) | copy-start | bytes 589828
  41.2 1.7 %copy-start.20 = (s32[256]{0:T(256)S(1)}, s32[256]{0:T(256)}, u32[]{:S(2)}) copy-start(s32[256]{0:T(256)} %param.26) | copy-start | bytes 3076
  43.0 26.7 %copy-start.3 = (bf16[1,768,1536]{2,1,0:T(8,128)(2,1)S(1)}, bf16[1,768,1536]{2,1,0:T(8,128)(2,1)}, u32[]{:S(2)}) copy-start(bf16[1,768,1536]{2,1,0:T(8,128)(2,1)} %refs_1_.1) | copy-start | bytes 7077892
  104.1 8.6 %copy-start.14 = (f32[256,768]{1,0:T(8,128)S(1)}, f32[256,768]{1,0:T(8,128)}, u32[]{:S(2)}) copy-start(f32[256,768]{1,0:T(8,128)} %get-tuple-element.63) | copy-start | bytes 2359300
  104.7 8.6 %copy-start.17 = (bf16[256,768]{1,0:T(8,128)(2,1)S(1)}, bf16[256,768]{1,0:T(8,128)(2,1)}, u32[]{:S(2)}) copy-start(bf16[256,768]{1,0:T(8,128)(2,1)} %param.29) | copy-start | bytes 1179652
  113.2 1.6 %copy-start.5 = (f32[6,256,256]{2,1,0:T(8,128)S(1)}, f32[6,256,256]{2,1,0:T(8,128)}, u32[]{:S(2)}) copy-start(f32[6,256,256]{2,1,0:T(8,128)} %copy-done.4) | copy-start | bytes 4718596
  113.2 1.8 %copy-start.7 = (bf16[3,256,384]{2,1,0:T(8,128)(2,1)S(1)}, bf16[3,256,384]{2,1,0:T(8,128)(2,1)}, u32[]{:S(2)}) copy-start(bf16[3,256,384]{2,1,0:T(8,128)(2,1)} %copy-done.6) | copy-start | bytes 1769476
  113.2 1.9 %copy-start.9 = (bf16[256,768]{1,0:T(8,128)(2,1)S(1)}, bf16[256,768]{1,0:T(8,128)(2,1)}, u32[]{:S(2)}) copy-start(bf16[256,768]{1,0:T(8,128)(2,1)} %copy-done.8) | copy-start | bytes 1179652
  113.2 2.0 %copy-start.11 = (bf16[256,384]{1,0:T(8,128)(2,1)S(1)}, bf16[256,384]{1,0:T(8,128)(2,1)}, u32[]{:S(2)}) copy-start(bf16[256,384]{1,0:T(8,128)(2,1)} %copy-done.10) | copy-start | bytes 589828
  121.3 33.8 %copy-start.19 = (f32[768]{0:T(1024)S(1)}, f32[768]{0:T(1024)}, u32[]{:S(2)}) copy-start(f32[768]{0:T(1024)} %param.21) | copy-start | bytes 9220
  122.0 33.1 %copy-start.15 = (f32[256,768]{1,0:T(8,128)S(1)}, f32[256,768]{1,0:T(8,128)}, u32[]{:S(2)}) copy-start(f32[256,768]{1,0:T(8,128)} %convert_element_type.46) | copy-start | bytes 2359300
  122.0 33.3 %copy-start.16 = (f32[256,768]{1,0:T(8,128)S(1)}, f32[256,768]{1,0:T(8,128)}, u32[]{:S(2)}) copy-start(f32[256,768]{1,0:T(8,128)} %get-tuple-element.59) | copy-start | bytes 2359300
  155.1 1.2 copy-start.12
  156.2 3.1 %copy-start.13 = (bf16[128,768]{1,0:T(8,128)(2,1)S(1)}, bf16[128,768]{1,0:T(8,128)(2,1)}, u32[]{:S(2)}) copy-start(bf16[128,768]{1,0:T(8,128)(2,1)} %copy-done.12) | copy-start | bytes 589828
